TPU v7x, 256 devices: a whole 4x4x8 slice. The times are simulated.
256 devices in a mesh: depth: 4 (over x_hi, core), rows: 64 (over y, x_lo, z).
Axes of the slice: x: 4 (x_hi: 2, x_lo: 2; x = x_hi * 2 + x_lo), y: 4, z: 8, core: 2. Of those that a mesh axis runs over, the one named last changes fastest.
Arguments:
- perturbation: float32 [8, 4096, 4096], P('depth', 'rows'), may hold values from -6 to 6
- level_set: float32 [8, 4096, 4096], P('depth', 'rows'), may hold values from -6 to 6
- labels: int32 [8, 4096, 4096], P('depth', 'rows'), may hold values from 0 to 3
- contrasts: float32 [4], replicated, may hold values from 0.8 to 4
- kernel: float32 [8, 4096, 4096], P('depth', 'rows'), may hold values from 0.3 to 1.5
Outputs:
- hessian_vector: float32 [8, 4096, 4096], P('depth', 'rows')
All inputs are finite; a program needn't handle non-finite values.
Results may differ from a plain program's by a relative error of at most 0.0001.
Values sent between devices are 32-bit elements; how exact they have to be, the bound alone decides.
No kernel may reach another device: no remote copies, remote signals or barrier semaphores. Data moves between devices by JAX's collectives and lax.ppermute only.
A program may use at most 128 MiB of HBM per device.

v0:
```python
import math

import jax
import jax.numpy as jnp
import ml_dtypes
import numpy as np
from jax import lax
from jax.experimental import pallas as pl
from jax.experimental.pallas import tpu as pltpu
from jax.sharding import PartitionSpec as P

smoothing = 0.5
length = 4096
chunks = 2
big = 60
bf16 = jnp.bfloat16


def cas(angle):
    return np.cos(angle) + np.sin(angle)


def stage_matrices(small, wide):
    b = np.arange(wide)[None, :]
    m = np.arange(wide)[:, None]
    turn = 2.0 * np.pi / wide
    low = np.concatenate([cas(turn * b * m), np.sin(turn * b * m) - np.cos(turn * b * m)], axis=1)
    high = np.concatenate(
        [cas(turn * b * (m + 1)), np.cos(turn * b * (m + 1)) - np.sin(turn * b * (m + 1))], axis=1
    )
    pair = np.concatenate([low, high], axis=0)
    first = np.zeros_like(pair)
    first[:wide, :wide] = cas(turn * b * m)
    full = 2.0 * np.pi / (small * wide)
    first[wide:, wide:] = cas(full * ((b * (small // 2 + small * m)) % (small * wide)))
    scale = 1.0 / math.sqrt(small * wide)
    return pair * scale, first * scale


def twiddles(small, wide):
    k = np.arange(small // 2)[:, None]
    b = np.arange(wide)[None, :]
    angle = 2.0 * np.pi / (small * wide) * k * b
    return np.stack([np.cos(angle), -np.sin(angle)], axis=1).astype(np.float32)


def split_matrix(matrix, axis):
    high = matrix.astype(ml_dtypes.bfloat16)
    low = (matrix - high.astype(np.float64)).astype(ml_dtypes.bfloat16)
    return np.concatenate([high, high, low], axis=axis)


def split_value(value, axis):
    high = value.astype(bf16)
    low = (value - high.astype(jnp.float32)).astype(bf16)
    return jnp.concatenate([high, low, high], axis=axis)


def dot(a, b, dims):
    return lax.dot_general(a, b, (dims, ((), ())), preferred_element_type=jnp.float32)


def real_fft(values):
    n = len(values)
    if n == 1:
        return [(values[0], None)]
    if n == 2:
        return [(values[0] + values[1], None), (values[0] - values[1], None)]
    even = real_fft(values[0::2])
    odd = real_fft(values[1::2])
    out = [None] * (n // 2 + 1)
    out[0] = (even[0][0] + odd[0][0], None)
    out[n // 2] = (even[0][0] - odd[0][0], None)
    out[n // 4] = (even[n // 4][0], -odd[n // 4][0])
    for k in range(1, n // 4):
        c, s = math.cos(2.0 * math.pi * k / n), math.sin(2.0 * math.pi * k / n)
        er, ei = even[k]
        orr, oi = odd[k]
        if 8 * k == n:
            tr, ti = (orr + oi) * c, (oi - orr) * c
        else:
            tr, ti = orr * c + oi * s, oi * c - orr * s
        out[k] = (er + tr, ei + ti)
        out[n // 2 - k] = (er - tr, ti - ei)
    return out


def real_fft_adjoint(spectrum):
    n = 2 * (len(spectrum) - 1)
    if n == 2:
        return [spectrum[0][0] + spectrum[1][0], spectrum[0][0] - spectrum[1][0]]
    even = [None] * (n // 4 + 1)
    odd = [None] * (n // 4 + 1)
    even[0] = (spectrum[0][0] + spectrum[n // 2][0], None)
    odd[0] = (spectrum[0][0] - spectrum[n // 2][0], None)
    even[n // 4] = (spectrum[n // 4][0], None)
    odd[n // 4] = (-spectrum[n // 4][1], None)
    for k in range(1, n // 4):
        c, s = math.cos(2.0 * math.pi * k / n), math.sin(2.0 * math.pi * k / n)
        ar, ai = spectrum[k]
        br, bi = spectrum[n // 2 - k]
        even[k] = (ar + br, ai - bi)
        dr, di = ar - br, ai + bi
        if 8 * k == n:
            odd[k] = ((dr - di) * c, (dr + di) * c)
        else:
            odd[k] = (dr * c - di * s, dr * s + di * c)
    out = [None] * n
    out[0::2] = real_fft_adjoint(even)
    out[1::2] = real_fft_adjoint(odd)
    return out


row_small, row_wide = 32, 128
col_small, col_wide = 64, 64
row_step = 32
steps = 128 // row_step


def row_forward(contrasts, labels, level_set, perturbation, turn, pair, first, weight, *rest):
    sends, parts = rest[:chunks], rest[chunks]
    step = pl.program_id(0)
    for tile in range(row_step // 8):
        rows = pl.ds(tile * 8, 8)
        fields = []
        for a in range(row_small):
            at = (rows, pl.ds(a * row_wide, row_wide))
            unit = labels[at]
            chosen = jnp.where(
                unit < 2,
                jnp.where(unit == 0, contrasts[0], contrasts[1]),
                jnp.where(unit == 2, contrasts[2], contrasts[3]),
            )
            level = level_set[at]
            here = chosen / (level * level + smoothing * smoothing)
            weight[at] = here
            fields.append(here * perturbation[at])
        spectrum = real_fft(fields)
        into = pl.ds(pl.multiple_of(step * row_step + tile * 8, 8), 8)
        parts[0, into, :row_wide] = spectrum[0][0]
        parts[0, into, row_wide:] = spectrum[row_small // 2][0]
        for k in range(1, row_small // 2):
            re, im = spectrum[k]
            c, s = turn[k, 0:1, :], turn[k, 1:2, :]
            parts[k, into, :row_wide] = re * c - im * s
            parts[k, into, row_wide:] = im * c + re * s

    @pl.when(step == steps - 1)
    def _():
        for k in range(row_small // 2):
            value = split_value(parts[k], 1)
            matrix = (pair if k else first)[...]
            out = dot(matrix, value, ((1,), (1,)))
            for half, place in enumerate((k, row_small - k if k else row_small // 2)):
                for chunk in range(chunks):
                    begin = (half * chunks + chunk) * 64
                    sends[chunk][pl.ds(place, 64, stride=row_small), :] = out[begin : begin + 64]


def row_backward(weight, received0, received1, turn, pair, first, out, parts):
    step = pl.program_id(0)
    received = (received0, received1)

    @pl.when(step == 0)
    def _():
        for k in range(row_small // 2):
            value = jnp.concatenate(
                [
                    received[chunk][pl.ds(place, 64, stride=row_small), :]
                    for place in (k, row_small - k if k else row_small // 2)
                    for chunk in range(chunks)
                ],
                axis=0,
            )
            value = split_value(value, 0)
            matrix = (pair if k else first)[...]
            parts[k] = dot(value, matrix, ((0,), (0,)))

    for tile in range(row_step // 8):
        rows = pl.ds(tile * 8, 8)
        source = pl.ds(pl.multiple_of(step * row_step + tile * 8, 8), 8)
        spectrum = [(parts[0, source, :row_wide], None)]
        for k in range(1, row_small // 2):
            tr, ti = parts[k, source, :row_wide], parts[k, source, row_wide:]
            c, s = turn[k, 0:1, :], turn[k, 1:2, :]
            spectrum.append((tr * c + ti * s, ti * c - tr * s))
        spectrum.append((parts[0, source, row_wide:], None))
        fields = real_fft_adjoint(spectrum)
        for a in range(row_small):
            at = (rows, pl.ds(a * row_wide, row_wide))
            out[at] = fields[a] * weight[at]


def column_forward(received, kernel, turn, pair, first, data, parts):
    spectrum = real_fft([received[r] for r in range(col_small)])
    parts[0, :, :128] = spectrum[0][0]
    parts[0, :, 128:] = spectrum[col_small // 2][0]
    for k in range(1, col_small // 2):
        re, im = spectrum[k]
        c, s = turn[k, 0:1, :], turn[k, 1:2, :]
        parts[k, :, :128] = re * c - im * s
        parts[k, :, 128:] = im * c + re * s
    half = col_small // 2
    value = split_value(parts[...].reshape(half * 8, 256), 1)
    rest = dot(value, pair[...], ((1,), (0,)))
    zero = dot(split_value(parts[0], 1), first[...], ((1,), (0,)))
    rest = rest.reshape(half, 8, 256)
    for k in range(half):
        spectra = (zero if k == 0 else rest[k]) * kernel[k]
        data[k] = spectra[:, :128] + spectra[:, 128:]


def column_backward(data, kernel, turn, pair, first, out, parts):
    half = col_small // 2
    both = jnp.concatenate([data[...], data[...]], axis=2)
    scaled = both * kernel[...]
    value = split_value(scaled.reshape(half * 8, 256), 1)
    parts[...] = dot(value, pair[...], ((1,), (0,))).reshape(half, 8, 256)
    parts[0] = dot(split_value(scaled[0], 1), first[...], ((1,), (0,)))
    spectrum = [(parts[0, :, :128], None)]
    for k in range(1, half):
        tr, ti = parts[k, :, :128], parts[k, :, 128:]
        c, s = turn[k, 0:1, :], turn[k, 1:2, :]
        spectrum.append((tr * c + ti * s, ti * c - tr * s))
    spectrum.append((parts[0, :, 128:], None))
    fields = real_fft_adjoint(spectrum)
    for r in range(col_small):
        out[r] = fields[r]


def whole(shape):
    return pl.BlockSpec(shape, lambda *_: (0,) * len(shape))


def params(mib):
    return pltpu.CompilerParams(vmem_limit_bytes=mib * 1024 * 1024)


def cost(flops, moved):
    return pl.CostEstimate(flops=flops, bytes_accessed=moved, transcendentals=0)


def column_matrices():
    out = []
    for matrix in stage_matrices(col_small, col_wide):
        both = np.zeros((2, 2, col_wide, 2, 2, col_wide))
        shaped = matrix.reshape(2, col_wide, 2, col_wide)
        for layer in range(2):
            both[layer, :, :, :, layer, :] = shaped
        out.append(both.reshape(256, 256))
    return out


def row_matrices():
    out = []
    for matrix in stage_matrices(row_small, row_wide):
        shaped = matrix.reshape(2, row_wide // chunks, chunks, 2 * row_wide)
        out.append(shaped.swapaxes(1, 2).reshape(256, 256))
    return out


def sum_over_depth(value):
    place = lax.axis_index("depth")
    core = place % 2
    swap_core = [(0, 1), (1, 0), (2, 3), (3, 2)]
    swap_chip = [(0, 2), (1, 3), (2, 0), (3, 1)]
    halves = value.reshape((2, value.shape[0] // 2) + value.shape[1:])
    mine = lax.dynamic_index_in_dim(halves, core, 0, keepdims=False)
    other = lax.dynamic_index_in_dim(halves, 1 - core, 0, keepdims=False)
    mine = mine + lax.ppermute(other, "depth", swap_core)
    mine = mine + lax.ppermute(mine, "depth", swap_chip)
    other = lax.ppermute(mine, "depth", swap_core)
    lower = jnp.where(core == 0, mine, other)
    upper = jnp.where(core == 0, other, mine)
    return jnp.concatenate([lower, upper], axis=0)


def kernel_in_pairs(kernel, *rest):
    outs, turned = rest[:chunks], rest[chunks]
    for tile in range(length // 128):
        lanes = pl.ds(tile * 128, 128)
        turned[lanes, :] = kernel[:, lanes].T
    for k in range(col_small // 2):
        places = (k, col_small - k if k else col_small // 2)
        pair = jnp.concatenate(
            [turned[pl.ds(place, col_wide, stride=col_small), :] for place in places], axis=0
        ).T
        for chunk in range(chunks):
            for layer in range(2):
                begin = layer * 64 + chunk * 32
                outs[chunk][k, :, layer * 128 : layer * 128 + 128] = pair[begin : begin + 32]


def on_device(perturbation, level_set, labels, contrasts, kernel):
    f32 = jnp.float32
    rows = [x.reshape(128, length) for x in (labels, level_set, perturbation)]
    scaled = contrasts * (smoothing / math.pi)
    row_turn = jnp.asarray(twiddles(row_small, row_wide))
    col_turn = twiddles(col_small, col_wide)
    col_turn = jnp.asarray(np.concatenate([col_turn, col_turn], axis=2))
    row_pair, row_first = row_matrices()
    col_pair, col_first = column_matrices()

    row_block = pl.BlockSpec((row_step, length), lambda i: (i, 0))
    sent = [(col_small * 32, 128)] * chunks
    weight, *sends = pl.pallas_call(
        row_forward,
        grid=(steps,),
        in_specs=[
            pl.BlockSpec(memory_space=pltpu.SMEM),
            row_block,
            row_block,
            row_block,
            whole((16, 2, 128)),
            whole((256, 768)),
            whole((256, 768)),
        ],
        out_specs=[row_block] + [whole(s) for s in sent],
        out_shape=[jax.ShapeDtypeStruct((128, length), f32)]
        + [jax.ShapeDtypeStruct(s, f32) for s in sent],
        scratch_shapes=[pltpu.VMEM((16, 128, 256), f32)],
        compiler_params=params(big),
        cost_estimate=cost(2 * 256 * 768 * 128 * 16, 12 * 2**20),
        name="row_forward",
    )(
        scaled,
        *rows,
        row_turn,
        jnp.asarray(split_matrix(row_pair, 1)),
        jnp.asarray(split_matrix(row_first, 1)),
    )

    kernels = pl.pallas_call(
        kernel_in_pairs,
        out_shape=[jax.ShapeDtypeStruct((32, 32, 256), f32)] * chunks,
        scratch_shapes=[pltpu.VMEM((length, 128), f32)],
        compiler_params=params(big),
        cost_estimate=cost(2 * 10**9, 4 * 2**20),
        name="kernel_in_pairs",
    )(kernel.reshape(128, length))

    tile = lambda n, lanes: pl.BlockSpec((n, 8, lanes), lambda i: (0, i, 0))
    mid = dict(grid=(4,), compiler_params=params(40))
    mid["cost_estimate"] = cost(2 * 768 * 256 * 1024, 5 * 2**19)
    mid["scratch_shapes"] = [pltpu.VMEM((32, 8, 256), f32)]
    constants = [whole((32, 2, 128)), whole((768, 256)), whole((768, 256))]
    forward = pl.pallas_call(
        column_forward,
        in_specs=[tile(64, 128), tile(32, 256)] + constants,
        out_specs=tile(32, 128),
        out_shape=jax.ShapeDtypeStruct((32, 32, 128), f32),
        name="column_forward",
        **mid,
    )
    backward = pl.pallas_call(
        column_backward,
        in_specs=[tile(32, 128), tile(32, 256)] + constants,
        out_specs=tile(64, 128),
        out_shape=jax.ShapeDtypeStruct((64, 32, 128), f32),
        name="column_backward",
        **mid,
    )
    forward_constants = [jnp.asarray(split_matrix(m.T, 0)) for m in (col_pair, col_first)]
    backward_constants = [jnp.asarray(split_matrix(m, 0)) for m in (col_pair, col_first)]

    returned = []
    for chunk in range(chunks):
        received = lax.all_to_all(
            sends[chunk].reshape(64, 32, 128), "rows", split_axis=0, concat_axis=0, tiled=True
        )
        local = forward(received, kernels[chunk], col_turn, *forward_constants)
        data = sum_over_depth(local)
        back = backward(data, kernels[chunk], col_turn, *backward_constants)
        back = lax.all_to_all(back, "rows", split_axis=0, concat_axis=0, tiled=True)
        returned.append(back.reshape(2048, 128))

    out = pl.pallas_call(
        row_backward,
        grid=(steps,),
        in_specs=[
            row_block,
            whole((2048, 128)),
            whole((2048, 128)),
            whole((16, 2, 128)),
            whole((768, 256)),
            whole((768, 256)),
        ],
        out_specs=row_block,
        out_shape=jax.ShapeDtypeStruct((128, length), f32),
        scratch_shapes=[pltpu.VMEM((16, 128, 256), f32)],
        compiler_params=params(big),
        cost_estimate=cost(2 * 256 * 768 * 128 * 16, 6 * 2**20),
        name="row_backward",
    )(
        weight,
        *returned,
        row_turn,
        jnp.asarray(split_matrix(row_pair, 0)),
        jnp.asarray(split_matrix(row_first, 0)),
    )
    return out.reshape(perturbation.shape)


def solution(mesh):
    in_specs = (
        P("depth", "rows", None),
        P("depth", "rows", None),
        P("depth", "rows", None),
        P(),
        P("depth", "rows", None),
    )
    out_specs = P("depth", "rows", None)
    return jax.shard_map(
        on_device, mesh=mesh, in_specs=in_specs, out_specs=out_specs, check_vma=False
    )
```

profile of v0, /device:TPU:32, one launch (start us, length us, event | category | flops | bytes accessed | tf_op | source)
XLA Modules:
  0.0 170.9 jit_solution(8730751348819920903)
XLA Ops:
  0.0 1.2 broadcast_multiply_fusion.contrasts
  1.2 8.9 %row_forward.1 = (f32[128,4096]{1,0:T(8,128)}, f32[2048,128]{1,0:T(8,128)}, f32[2048,128]{1,0:T(8,128)}) custom-call(f32[4]{0:T(128)} %broadcast_multiply_fusion.contrasts, s32[128,4096]{1,0:T(8,128)} %bitcast.24, f32[128,4096]{1,0:T(8,128)} %bitcast.25, f32[128,4096]{1,0:T(8,128)} %bitcast.26, f32[16,2,128]{2,1,0:T(2,128)} %constant.57.clone.turn, ...), custom_call_target="tpu_custom_call" | custom-call | flops 805306368 | bytes 12582912 | tf_op jit(solution)/shard_map/row_forward/pallas_call | solution.py:306
  10.1 41.9 %all_to_all.20.received = f32[64,32,128]{2,1,0:T(8,128)S(1)} all-to-all(f32[64,32,128]{2,1,0:T(8,128)} %bitcast.27), channel_id=1, replica_groups=mesh['depth'=4,'rows'=64] {'rows'}, dimensions={0} | all-to-all | bytes 2097152 | tf_op jit(solution)/shard_map/all_to_all | solution.py:368
  52.0 5.8 %all-to-all-start = ((f32[64,32,128]{2,1,0:T(8,128)}), f32[64,32,128]{2,1,0:T(8,128)S(1)}, u32[]{:S(2)}, u32[]{:S(2)}) async-start(f32[64,32,128]{2,1,0:T(8,128)} %bitcast.3), calls=%async_computation | async-start | bytes 2097152 | tf_op jit(solution)/shard_map/all_to_all | solution.py:368
  57.9 4.7 %kernel_in_pairs.1 = (f32[32,32,256]{2,1,0:T(8,128)}, f32[32,32,256]{2,1,0:T(8,128)}) custom-call(f32[128,4096]{1,0:T(8,128)} %bitcast.28), custom_call_target="tpu_custom_call" | custom-call | flops 2000000000 | bytes 4194304 | tf_op jit(solution)/shard_map/kernel_in_pairs/pallas_call | solution.py:333
  62.6 1.2 copy-done.1
  63.8 1.8 %column_forward.3 = f32[32,32,128]{2,1,0:T(8,128)S(1)} custom-call(f32[64,32,128]{2,1,0:T(8,128)S(1)} %all_to_all.20.received, f32[32,32,256]{2,1,0:T(8,128)S(1)} %copy-done.1, f32[32,2,128]{2,1,0:T(2,128)S(1)} %copy-done.11, bf16[768,256]{1,0:T(8,128)(2,1)S(1)} %copy-done.7, bf16[768,256]{1,0:T(8,128)(2,1)S(1)} %copy-done.9), custom_call_target="tpu_custom_call" | custom-call | flops 402653184 | bytes 2621440 | tf_op jit(solution)/shard_map/column_forward/pallas_call | solution.py:371
  66.5 1.5 collective-permute-done.3
  68.1 1.0 bitcast_add_fusion
  69.0 2.8 %collective-permute-start.4 = (f32[16,32,128]{2,1,0:T(8,128)S(1)}, f32[16,32,128]{2,1,0:T(8,128)S(1)}, u32[]{:S(2)}, u32[]{:S(2)}) collective-permute-start(f32[16,32,128]{2,1,0:T(8,128)S(1)} %bitcast_add_fusion), channel_id=1, source_target_pairs={{0,128},{64,192},{128,0},{192,64},{1,129},{65,193},{129,1},{193,65... | collective-permute-start | bytes 786440 | tf_op jit(solution)/shard_map/ppermute | solution.py:271
  71.9 11.5 %collective-permute-done.4 = f32[16,32,128]{2,1,0:T(8,128)S(1)} collective-permute-done((f32[16,32,128]{2,1,0:T(8,128)S(1)}, f32[16,32,128]{2,1,0:T(8,128)S(1)}, u32[]{:S(2)}, u32[]{:S(2)}) %collective-permute-start.4) | collective-permute-done | bytes 262176 | tf_op jit(solution)/shard_map/ppermute | solution.py:271
  83.5 1.5 collective-permute-done.5
  85.1 1.0 copy-done.5
  86.9 2.8 %column_backward.3 = f32[64,32,128]{2,1,0:T(8,128)} custom-call(f32[32,32,128]{2,1,0:T(8,128)S(1)} %pad_maximum_fusion.1.data, f32[32,32,256]{2,1,0:T(8,128)S(1)} %copy-done.2, f32[32,2,128]{2,1,0:T(2,128)S(1)} %copy-done.12, bf16[768,256]{1,0:T(8,128)(2,1)S(1)} %copy-done.4, bf16[768,256]{1,0:T(8,128)(2,1)S(1)} %copy-done.5), custom_call_target="tpu_custom_call" | custom-call | flops 402653184 | bytes 2621440 | tf_op jit(solution)/shard_map/column_backward/pallas_call | solution.py:373
  89.7 10.6 %all-to-all-start.3 = ((f32[64,32,128]{2,1,0:T(8,128)}), f32[64,32,128]{2,1,0:T(8,128)}, u32[]{:S(2)}, u32[]{:S(2)}) async-start(f32[64,32,128]{2,1,0:T(8,128)} %column_backward.3), calls=%async_computation.3 | async-start | bytes 2097152 | tf_op jit(solution)/shard_map/all_to_all | solution.py:374
  100.3 1.8 %column_forward.2 = f32[32,32,128]{2,1,0:T(8,128)S(1)} custom-call(f32[64,32,128]{2,1,0:T(8,128)S(1)} %all-to-all-done.received, f32[32,32,256]{2,1,0:T(8,128)S(1)} %copy-done, f32[32,2,128]{2,1,0:T(2,128)S(1)} %copy-done.13, bf16[768,256]{1,0:T(8,128)(2,1)S(1)} %copy-done.8, bf16[768,256]{1,0:T(8,128)(2,1)S(1)} %copy-done.10), custom_call_target="tpu_custom_call" | custom-call | flops 402653184 | bytes 2621440 | tf_op jit(solution)/shard_map/column_forward/pallas_call | solution.py:371
  102.3 1.5 collective-permute-done
  103.8 2.6 %collective-permute-start.1 = (f32[16,32,128]{2,1,0:T(8,128)S(1)}, f32[16,32,128]{2,1,0:T(8,128)S(1)}, u32[]{:S(2)}, u32[]{:S(2)}) collective-permute-start(f32[16,32,128]{2,1,0:T(8,128)S(1)} %bitcast_add_fusion.1), channel_id=1, source_target_pairs={{0,128},{64,192},{128,0},{192,64},{1,129},{65,193},{129,1},{193,65... | collective-permute-start | bytes 786440 | tf_op jit(solution)/shard_map/ppermute | solution.py:271
  106.4 11.4 %collective-permute-done.1 = f32[16,32,128]{2,1,0:T(8,128)S(1)} collective-permute-done((f32[16,32,128]{2,1,0:T(8,128)S(1)}, f32[16,32,128]{2,1,0:T(8,128)S(1)}, u32[]{:S(2)}, u32[]{:S(2)}) %collective-permute-start.1) | collective-permute-done | bytes 262176 | tf_op jit(solution)/shard_map/ppermute | solution.py:271
  118.1 1.5 collective-permute-done.2
  119.8 1.9 %column_backward.2 = f32[64,32,128]{2,1,0:T(8,128)S(1)} custom-call(f32[32,32,128]{2,1,0:T(8,128)S(1)} %pad_maximum_fusion.data, f32[32,32,256]{2,1,0:T(8,128)S(1)} %copy-done, f32[32,2,128]{2,1,0:T(2,128)S(1)} %copy-done.13, bf16[768,256]{1,0:T(8,128)(2,1)S(1)} %copy-done.4, bf16[768,256]{1,0:T(8,128)(2,1)S(1)} %copy-done.6), custom_call_target="tpu_custom_call" | custom-call | flops 402653184 | bytes 2621440 | tf_op jit(solution)/shard_map/column_backward/pallas_call | solution.py:373
  121.6 8.1 %all-to-all-done.3 = f32[64,32,128]{2,1,0:T(8,128)} async-done(((f32[64,32,128]{2,1,0:T(8,128)}), f32[64,32,128]{2,1,0:T(8,128)}, u32[]{:S(2)}, u32[]{:S(2)}) %all-to-all-start.3) | async-done | bytes 1048608 | tf_op jit(solution)/shard_map/all_to_all | solution.py:374
  129.7 34.2 %all_to_all.21 = f32[64,32,128]{2,1,0:T(8,128)} all-to-all(f32[64,32,128]{2,1,0:T(8,128)S(1)} %column_backward.2), channel_id=1, replica_groups=mesh['depth'=4,'rows'=64] {'rows'}, dimensions={0} | all-to-all | bytes 2097152 | tf_op jit(solution)/shard_map/all_to_all | solution.py:374
  163.9 6.9 %row_backward.1 = f32[128,4096]{1,0:T(8,128)} custom-call(f32[128,4096]{1,0:T(8,128)} %get-tuple-element.10.weight, f32[2048,128]{1,0:T(8,128)} %bitcast.23, f32[2048,128]{1,0:T(8,128)} %bitcast.13.received1, f32[16,2,128]{2,1,0:T(2,128)} %constant.57.clone.turn, bf16[768,256]{1,0:T(8,128)(2,1)} %constant.65.clone.pair, bf16[768,256]{1,0:T(8,128)(2,1)} %constant.66.clone.first), custom_call_target="tpu_custom_call" | custom-call | flops 805306368 | bytes 6291456 | tf_op jit(solution)/shard_map/row_backward/pallas_call | solution.py:377
  (40 shorter events, 2.5 us)
Async XLA Ops:
  52.0 37.6 %all-to-all-start = ((f32[64,32,128]{2,1,0:T(8,128)}), f32[64,32,128]{2,1,0:T(8,128)S(1)}, u32[]{:S(2)}, u32[]{:S(2)}) async-start(f32[64,32,128]{2,1,0:T(8,128)} %bitcast.3), calls=%async_computation | async-start | bytes 2097152 | tf_op jit(solution)/shard_map/all_to_all | solution.py:368
  57.9 4.7 %copy-start.7 = (bf16[768,256]{1,0:T(8,128)(2,1)S(1)}, bf16[768,256]{1,0:T(8,128)(2,1)}, u32[]{:S(2)}) copy-start(bf16[768,256]{1,0:T(8,128)(2,1)} %constant.61.clone.pair) | copy-start | bytes 1179652
  57.9 4.7 %copy-start.9 = (bf16[768,256]{1,0:T(8,128)(2,1)S(1)}, bf16[768,256]{1,0:T(8,128)(2,1)}, u32[]{:S(2)}) copy-start(bf16[768,256]{1,0:T(8,128)(2,1)} %constant.62.clone.first) | copy-start | bytes 1179652
  57.9 4.7 %copy-start.11 = (f32[32,2,128]{2,1,0:T(2,128)S(1)}, f32[32,2,128]{2,1,0:T(2,128)}, u32[]{:S(2)}) copy-start(f32[32,2,128]{2,1,0:T(2,128)} %constant.58.clone.turn) | copy-start | bytes 98308
  62.6 1.2 copy-start.1
  65.6 0.8 copy-start.3
  66.4 18.7 %copy-start.2 = (f32[32,32,256]{2,1,0:T(8,128)S(1)}, f32[32,32,256]{2,1,0:T(8,128)}, u32[]{:S(2)}) copy-start(f32[32,32,256]{2,1,0:T(8,128)} %get-tuple-element.14.kernel) | copy-start | bytes 3145732
  66.4 18.7 %copy-start.4 = (bf16[768,256]{1,0:T(8,128)(2,1)S(1)}, bf16[768,256]{1,0:T(8,128)(2,1)}, u32[]{:S(2)}) copy-start(bf16[768,256]{1,0:T(8,128)(2,1)} %constant.63.clone.pair) | copy-start | bytes 1179652
  66.4 1.6 collective-permute-start.3
  69.0 14.3 %collective-permute-start.4 = (f32[16,32,128]{2,1,0:T(8,128)S(1)}, f32[16,32,128]{2,1,0:T(8,128)S(1)}, u32[]{:S(2)}, u32[]{:S(2)}) collective-permute-start(f32[16,32,128]{2,1,0:T(8,128)S(1)} %bitcast_add_fusion), channel_id=1, source_target_pairs={{0,128},{64,192},{128,0},{192,64},{1,129},{65,193},{129,1},{193,65... | collective-permute-start | bytes 786440 | tf_op jit(solution)/shard_map/ppermute | solution.py:271
  83.4 1.6 collective-permute-start.5
  85.1 1.0 copy-start.5
  86.1 0.8 copy-start.12
  86.9 13.4 %copy-start = (f32[32,32,256]{2,1,0:T(8,128)S(1)}, f32[32,32,256]{2,1,0:T(8,128)}, u32[]{:S(2)}) copy-start(f32[32,32,256]{2,1,0:T(8,128)} %get-tuple-element.12.kernel) | copy-start | bytes 3145732
  89.6 10.7 %copy-start.8 = (bf16[768,256]{1,0:T(8,128)(2,1)S(1)}, bf16[768,256]{1,0:T(8,128)(2,1)}, u32[]{:S(2)}) copy-start(bf16[768,256]{1,0:T(8,128)(2,1)} %constant.61.clone.pair) | copy-start | bytes 1179652
  89.6 10.7 %copy-start.10 = (bf16[768,256]{1,0:T(8,128)(2,1)S(1)}, bf16[768,256]{1,0:T(8,128)(2,1)}, u32[]{:S(2)}) copy-start(bf16[768,256]{1,0:T(8,128)(2,1)} %constant.62.clone.first) | copy-start | bytes 1179652
  89.6 10.7 %copy-start.13 = (f32[32,2,128]{2,1,0:T(2,128)S(1)}, f32[32,2,128]{2,1,0:T(2,128)}, u32[]{:S(2)}) copy-start(f32[32,2,128]{2,1,0:T(2,128)} %constant.58.clone.turn) | copy-start | bytes 98308
  89.7 40.0 %all-to-all-start.3 = ((f32[64,32,128]{2,1,0:T(8,128)}), f32[64,32,128]{2,1,0:T(8,128)}, u32[]{:S(2)}, u32[]{:S(2)}) async-start(f32[64,32,128]{2,1,0:T(8,128)} %column_backward.3), calls=%async_computation.3 | async-start | bytes 2097152 | tf_op jit(solution)/shard_map/all_to_all | solution.py:374
  102.1 17.6 %copy-start.6 = (bf16[768,256]{1,0:T(8,128)(2,1)S(1)}, bf16[768,256]{1,0:T(8,128)(2,1)}, u32[]{:S(2)}) copy-start(bf16[768,256]{1,0:T(8,128)(2,1)} %constant.64.clone.first) | copy-start | bytes 1179652
  102.2 1.6 collective-permute-start
  103.8 14.0 %collective-permute-start.1 = (f32[16,32,128]{2,1,0:T(8,128)S(1)}, f32[16,32,128]{2,1,0:T(8,128)S(1)}, u32[]{:S(2)}, u32[]{:S(2)}) collective-permute-start(f32[16,32,128]{2,1,0:T(8,128)S(1)} %bitcast_add_fusion.1), channel_id=1, source_target_pairs={{0,128},{64,192},{128,0},{192,64},{1,129},{65,193},{129,1},{193,65... | collective-permute-start | bytes 786440 | tf_op jit(solution)/shard_map/ppermute | solution.py:271
  117.9 1.8 %collective-permute-start.2 = (f32[16,32,128]{2,1,0:T(8,128)S(1)}, f32[16,32,128]{2,1,0:T(8,128)S(1)}, u32[]{:S(2)}, u32[]{:S(2)}) collective-permute-start(f32[16,32,128]{2,1,0:T(8,128)S(1)} %add.31), channel_id=1, source_target_pairs={{0,64},{64,0},{128,192},{192,128},{1,65},{65,1},{129,193},{193,129... | collective-permute-start | bytes 786440 | tf_op jit(solution)/shard_map/ppermute | solution.py:272
where the time goes:
time: 172 us; the launch traced here: 171 us
  blocking collectives  76.2 us (44%)
  waiting for transfers between devices  37 us (22%)
  Pallas kernels  28.7 us (17%)
  starting transfers between devices  22.4 us (13%)
  local copies, waits for them, and re-layouts  3.85 us (2%)
  other arithmetic  2.43 us (1%)
    all_to_all x1, blocking collectives, on_device(): lax.all_to_all(sends[chunk].reshape(64, 32, 128), 'rows', split_axis=0, c...  41.9 us
    all_to_all x1, blocking collectives, on_device(): back = lax.all_to_all(back, 'rows', split_axis=0, concat_axis=0, tiled=True)  34.2 us
    ppermute x2, waiting for transfers between devices, sum_over_depth(): mine = mine + lax.ppermute(mine, 'depth', swap_chip)  22.8 us
    all_to_all x1, starting transfers between devices, on_device(): back = lax.all_to_all(back, 'rows', split_axis=0, concat_axis=0, tiled=True)  10.6 us
    pallas_call x1, Pallas kernels, on_device(): pl.pallas_call(row_forward, grid=(steps,), in_specs=[pl.BlockSpec(memory_...  8.9 us
    all_to_all x1, waiting for transfers between devices, on_device(): back = lax.all_to_all(back, 'rows', split_axis=0, concat_axis=0, tiled=True)  8.08 us
    pallas_call x1, Pallas kernels, on_device(): pl.pallas_call(row_backward, grid=(steps,), in_specs=[row_block, whole((2...  6.91 us
    all_to_all x1, starting transfers between devices, on_device(): lax.all_to_all(sends[chunk].reshape(64, 32, 128), 'rows', split_axis=0, c...  5.82 us
  transfers between devices with their start and end apart: 8, of which 7 were waited for; matrix products, arithmetic and copies ran while one was open for 1% of the time, Pallas kernels for 8%

commit v1 on v0

--- a/solution.py
+++ b/solution.py
@@ -11,7 +11,6 @@
 
 smoothing = 0.5
 length = 4096
-chunks = 2
 big = 60
 bf16 = jnp.bfloat16
 
@@ -117,9 +116,13 @@
 steps = 128 // row_step
 
 
-def row_forward(contrasts, labels, level_set, perturbation, turn, pair, first, weight, *rest):
-    sends, parts = rest[:chunks], rest[chunks]
+def block_rows(k, odd):
+    return pl.ds((2 * odd + k // 16) * 64 * 16 + k % 16, 64, stride=16)
+
+
+def row_forward(contrasts, labels, level_set, perturbation, turn, pair, first, weight, send, parts):
     step = pl.program_id(0)
+    scaled = [contrasts[unit] * (smoothing / math.pi) for unit in range(4)]
     for tile in range(row_step // 8):
         rows = pl.ds(tile * 8, 8)
         fields = []
@@ -128,8 +131,8 @@
             unit = labels[at]
             chosen = jnp.where(
                 unit < 2,
-                jnp.where(unit == 0, contrasts[0], contrasts[1]),
-                jnp.where(unit == 2, contrasts[2], contrasts[3]),
+                jnp.where(unit == 0, scaled[0], scaled[1]),
+                jnp.where(unit == 2, scaled[2], scaled[3]),
             )
             level = level_set[at]
             here = chosen / (level * level + smoothing * smoothing)
@@ -152,23 +155,22 @@
             matrix = (pair if k else first)[...]
             out = dot(matrix, value, ((1,), (1,)))
             for half, place in enumerate((k, row_small - k if k else row_small // 2)):
-                for chunk in range(chunks):
-                    begin = (half * chunks + chunk) * 64
-                    sends[chunk][pl.ds(place, 64, stride=row_small), :] = out[begin : begin + 64]
-
-
-def row_backward(weight, received0, received1, turn, pair, first, out, parts):
+                for odd in range(2):
+                    begin = (half * 2 + odd) * 64
+                    send[block_rows(place, odd), :] = out[begin : begin + 64]
+
+
+def row_backward(weight, received, turn, pair, first, out, parts):
     step = pl.program_id(0)
-    received = (received0, received1)
 
     @pl.when(step == 0)
     def _():
         for k in range(row_small // 2):
             value = jnp.concatenate(
                 [
-                    received[chunk][pl.ds(place, 64, stride=row_small), :]
+                    received[block_rows(place, odd), :]
                     for place in (k, row_small - k if k else row_small // 2)
-                    for chunk in range(chunks)
+                    for odd in range(2)
                 ],
                 axis=0,
             )
@@ -191,41 +193,39 @@
             out[at] = fields[a] * weight[at]
 
 
-def column_forward(received, kernel, turn, pair, first, data, parts):
-    spectrum = real_fft([received[r] for r in range(col_small)])
-    parts[0, :, :128] = spectrum[0][0]
-    parts[0, :, 128:] = spectrum[col_small // 2][0]
-    for k in range(1, col_small // 2):
-        re, im = spectrum[k]
-        c, s = turn[k, 0:1, :], turn[k, 1:2, :]
-        parts[k, :, :128] = re * c - im * s
-        parts[k, :, 128:] = im * c + re * s
+def column(place, received, kernel, turn, pair, first, pair_back, first_back, out, parts, data):
     half = col_small // 2
-    value = split_value(parts[...].reshape(half * 8, 256), 1)
-    rest = dot(value, pair[...], ((1,), (0,)))
-    zero = dot(split_value(parts[0], 1), first[...], ((1,), (0,)))
-    rest = rest.reshape(half, 8, 256)
-    for k in range(half):
-        spectra = (zero if k == 0 else rest[k]) * kernel[k]
-        data[k] = spectra[:, :128] + spectra[:, 128:]
-
-
-def column_backward(data, kernel, turn, pair, first, out, parts):
-    half = col_small // 2
-    both = jnp.concatenate([data[...], data[...]], axis=2)
-    scaled = both * kernel[...]
-    value = split_value(scaled.reshape(half * 8, 256), 1)
-    parts[...] = dot(value, pair[...], ((1,), (0,))).reshape(half, 8, 256)
-    parts[0] = dot(split_value(scaled[0], 1), first[...], ((1,), (0,)))
-    spectrum = [(parts[0, :, :128], None)]
-    for k in range(1, half):
-        tr, ti = parts[k, :, :128], parts[k, :, 128:]
-        c, s = turn[k, 0:1, :], turn[k, 1:2, :]
-        spectrum.append((tr * c + ti * s, ti * c - tr * s))
-    spectrum.append((parts[0, :, 128:], None))
-    fields = real_fft_adjoint(spectrum)
-    for r in range(col_small):
-        out[r] = fields[r]
+    for e in range(4):
+        source = place[0] ^ e
+        spectrum = real_fft([received[source, r] for r in range(col_small)])
+        parts[e, 0, :, :128] = spectrum[0][0]
+        parts[e, 0, :, 128:] = spectrum[half][0]
+        for k in range(1, half):
+            re, im = spectrum[k]
+            c, s = turn[k, 0:1, :], turn[k, 1:2, :]
+            parts[e, k, :, :128] = re * c - im * s
+            parts[e, k, :, 128:] = im * c + re * s
+        rest = dot(split_value(parts[e].reshape(half * 8, 256), 1), pair[...], ((1,), (0,)))
+        zero = dot(split_value(parts[e, 0], 1), first[...], ((1,), (0,)))
+        rest = rest.reshape(half, 8, 256)
+        for k in range(half):
+            spectra = (zero if k == 0 else rest[k]) * kernel[e, k]
+            spectra = spectra[:, :128] + spectra[:, 128:]
+            data[k] = spectra if e == 0 else data[k] + spectra
+    for e in range(4):
+        scaled = jnp.concatenate([data[...], data[...]], axis=2) * kernel[e]
+        value = split_value(scaled.reshape(half * 8, 256), 1)
+        parts[e] = dot(value, pair_back[...], ((1,), (0,))).reshape(half, 8, 256)
+        parts[e, 0] = dot(split_value(scaled[0], 1), first_back[...], ((1,), (0,)))
+        spectrum = [(parts[e, 0, :, :128], None)]
+        for k in range(1, half):
+            tr, ti = parts[e, k, :, :128], parts[e, k, :, 128:]
+            c, s = turn[k, 0:1, :], turn[k, 1:2, :]
+            spectrum.append((tr * c + ti * s, ti * c - tr * s))
+        spectrum.append((parts[e, 0, :, 128:], None))
+        fields = real_fft_adjoint(spectrum)
+        for r in range(col_small):
+            out[place[0] ^ e, r] = fields[r]
 
 
 def whole(shape):
@@ -254,47 +254,41 @@
 def row_matrices():
     out = []
     for matrix in stage_matrices(row_small, row_wide):
-        shaped = matrix.reshape(2, row_wide // chunks, chunks, 2 * row_wide)
+        shaped = matrix.reshape(2, row_wide // 2, 2, 2 * row_wide)
         out.append(shaped.swapaxes(1, 2).reshape(256, 256))
     return out
 
 
-def sum_over_depth(value):
-    place = lax.axis_index("depth")
-    core = place % 2
-    swap_core = [(0, 1), (1, 0), (2, 3), (3, 2)]
-    swap_chip = [(0, 2), (1, 3), (2, 0), (3, 1)]
-    halves = value.reshape((2, value.shape[0] // 2) + value.shape[1:])
-    mine = lax.dynamic_index_in_dim(halves, core, 0, keepdims=False)
-    other = lax.dynamic_index_in_dim(halves, 1 - core, 0, keepdims=False)
-    mine = mine + lax.ppermute(other, "depth", swap_core)
-    mine = mine + lax.ppermute(mine, "depth", swap_chip)
-    other = lax.ppermute(mine, "depth", swap_core)
-    lower = jnp.where(core == 0, mine, other)
-    upper = jnp.where(core == 0, other, mine)
-    return jnp.concatenate([lower, upper], axis=0)
-
-
-def kernel_in_pairs(kernel, *rest):
-    outs, turned = rest[:chunks], rest[chunks]
+def kernel_in_pairs(*refs):
+    sources, out, turned = refs[:4], refs[4], refs[5]
     for tile in range(length // 128):
         lanes = pl.ds(tile * 128, 128)
-        turned[lanes, :] = kernel[:, lanes].T
+        turned[lanes, :] = jnp.concatenate([x[:, lanes] for x in sources], axis=0).T
     for k in range(col_small // 2):
         places = (k, col_small - k if k else col_small // 2)
         pair = jnp.concatenate(
             [turned[pl.ds(place, col_wide, stride=col_small), :] for place in places], axis=0
         ).T
-        for chunk in range(chunks):
+        for e in range(4):
             for layer in range(2):
-                begin = layer * 64 + chunk * 32
-                outs[chunk][k, :, layer * 128 : layer * 128 + 128] = pair[begin : begin + 32]
+                begin = e * 32 + layer * 16
+                out[e, k, :, layer * 128 : layer * 128 + 128] = pair[begin : begin + 16]
+
+
+def exchange_kernel(kernel):
+    place = lax.axis_index("depth")
+    out = []
+    for e in range(4):
+        block = lax.dynamic_slice_in_dim(kernel, (place ^ e) * 16, 16, axis=1)
+        if e:
+            block = lax.ppermute(block, "depth", [(d, d ^ e) for d in range(4)])
+        out.append(block.reshape(32, length))
+    return out
 
 
 def on_device(perturbation, level_set, labels, contrasts, kernel):
     f32 = jnp.float32
     rows = [x.reshape(128, length) for x in (labels, level_set, perturbation)]
-    scaled = contrasts * (smoothing / math.pi)
     row_turn = jnp.asarray(twiddles(row_small, row_wide))
     col_turn = twiddles(col_small, col_wide)
     col_turn = jnp.asarray(np.concatenate([col_turn, col_turn], axis=2))
@@ -302,8 +296,7 @@
     col_pair, col_first = column_matrices()
 
     row_block = pl.BlockSpec((row_step, length), lambda i: (i, 0))
-    sent = [(col_small * 32, 128)] * chunks
-    weight, *sends = pl.pallas_call(
+    weight, send = pl.pallas_call(
         row_forward,
         grid=(steps,),
         in_specs=[
@@ -315,72 +308,71 @@
             whole((256, 768)),
             whole((256, 768)),
         ],
-        out_specs=[row_block] + [whole(s) for s in sent],
-        out_shape=[jax.ShapeDtypeStruct((128, length), f32)]
-        + [jax.ShapeDtypeStruct(s, f32) for s in sent],
+        out_specs=[row_block, whole((length, 128))],
+        out_shape=[
+            jax.ShapeDtypeStruct((128, length), f32),
+            jax.ShapeDtypeStruct((length, 128), f32),
+        ],
         scratch_shapes=[pltpu.VMEM((16, 128, 256), f32)],
         compiler_params=params(big),
         cost_estimate=cost(2 * 256 * 768 * 128 * 16, 12 * 2**20),
         name="row_forward",
     )(
-        scaled,
+        contrasts,
         *rows,
         row_turn,
         jnp.asarray(split_matrix(row_pair, 1)),
         jnp.asarray(split_matrix(row_first, 1)),
     )
 
+    send, kernel = lax.optimization_barrier((send, kernel))
+    received = lax.all_to_all(
+        send.reshape(256, 16, 128), ("depth", "rows"), split_axis=0, concat_axis=0, tiled=True
+    )
     kernels = pl.pallas_call(
         kernel_in_pairs,
-        out_shape=[jax.ShapeDtypeStruct((32, 32, 256), f32)] * chunks,
+        out_shape=jax.ShapeDtypeStruct((4, 32, 16, 256), f32),
         scratch_shapes=[pltpu.VMEM((length, 128), f32)],
-        compiler_params=params(big),
+        compiler_params=params(16),
         cost_estimate=cost(2 * 10**9, 4 * 2**20),
         name="kernel_in_pairs",
-    )(kernel.reshape(128, length))
-
-    tile = lambda n, lanes: pl.BlockSpec((n, 8, lanes), lambda i: (0, i, 0))
-    mid = dict(grid=(4,), compiler_params=params(40))
-    mid["cost_estimate"] = cost(2 * 768 * 256 * 1024, 5 * 2**19)
-    mid["scratch_shapes"] = [pltpu.VMEM((32, 8, 256), f32)]
-    constants = [whole((32, 2, 128)), whole((768, 256)), whole((768, 256))]
-    forward = pl.pallas_call(
-        column_forward,
-        in_specs=[tile(64, 128), tile(32, 256)] + constants,
-        out_specs=tile(32, 128),
-        out_shape=jax.ShapeDtypeStruct((32, 32, 128), f32),
-        name="column_forward",
-        **mid,
-    )
-    backward = pl.pallas_call(
-        column_backward,
-        in_specs=[tile(32, 128), tile(32, 256)] + constants,
-        out_specs=tile(64, 128),
-        out_shape=jax.ShapeDtypeStruct((64, 32, 128), f32),
-        name="column_backward",
-        **mid,
-    )
-    forward_constants = [jnp.asarray(split_matrix(m.T, 0)) for m in (col_pair, col_first)]
-    backward_constants = [jnp.asarray(split_matrix(m, 0)) for m in (col_pair, col_first)]
-
-    returned = []
-    for chunk in range(chunks):
-        received = lax.all_to_all(
-            sends[chunk].reshape(64, 32, 128), "rows", split_axis=0, concat_axis=0, tiled=True
-        )
-        local = forward(received, kernels[chunk], col_turn, *forward_constants)
-        data = sum_over_depth(local)
-        back = backward(data, kernels[chunk], col_turn, *backward_constants)
-        back = lax.all_to_all(back, "rows", split_axis=0, concat_axis=0, tiled=True)
-        returned.append(back.reshape(2048, 128))
+    )(*exchange_kernel(kernel))
+
+    block = pl.BlockSpec((4, 64, 8, 128), lambda i: (0, 0, i, 0))
+    back = pl.pallas_call(
+        column,
+        grid=(2,),
+        in_specs=[
+            pl.BlockSpec(memory_space=pltpu.SMEM),
+            block,
+            pl.BlockSpec((4, 32, 8, 256), lambda i: (0, 0, i, 0)),
+            whole((32, 2, 128)),
+        ]
+        + [whole((768, 256))] * 4,
+        out_specs=block,
+        out_shape=jax.ShapeDtypeStruct((4, 64, 16, 128), f32),
+        scratch_shapes=[pltpu.VMEM((4, 32, 8, 256), f32), pltpu.VMEM((32, 8, 128), f32)],
+        compiler_params=params(32),
+        cost_estimate=cost(2 * 768 * 256 * 4096, 6 * 2**20),
+        name="column",
+    )(
+        lax.axis_index("depth").reshape(1),
+        received.reshape(4, 64, 16, 128),
+        kernels,
+        col_turn,
+        *[jnp.asarray(split_matrix(m.T, 0)) for m in (col_pair, col_first)],
+        *[jnp.asarray(split_matrix(m, 0)) for m in (col_pair, col_first)],
+    )
+    returned = lax.all_to_all(
+        back.reshape(256, 16, 128), ("depth", "rows"), split_axis=0, concat_axis=0, tiled=True
+    )
 
     out = pl.pallas_call(
         row_backward,
         grid=(steps,),
         in_specs=[
             row_block,
-            whole((2048, 128)),
-            whole((2048, 128)),
+            whole((length, 128)),
             whole((16, 2, 128)),
             whole((768, 256)),
             whole((768, 256)),
@@ -388,12 +380,12 @@
         out_specs=row_block,
         out_shape=jax.ShapeDtypeStruct((128, length), f32),
         scratch_shapes=[pltpu.VMEM((16, 128, 256), f32)],
-        compiler_params=params(big),
+        compiler_params=params(24),
         cost_estimate=cost(2 * 256 * 768 * 128 * 16, 6 * 2**20),
         name="row_backward",
     )(
         weight,
-        *returned,
+        returned.reshape(length, 128),
         row_turn,
         jnp.asarray(split_matrix(row_pair, 0)),
         jnp.asarray(split_matrix(row_first, 0)),

time: 172 us -> 151 us (0.88)
  blocking collectives: 76.2 us -> 62.8 us
  Pallas kernels: 28.7 us -> 17.6 us
  waiting for transfers between devices: 37 us -> 45.7 us
  starting transfers between devices: 22.4 us -> 17.8 us
  other arithmetic: 2.43 us -> 0 us
  local copies, waits for them, and re-layouts: 3.85 us -> 5.63 us
    all_to_all x2 -> x1, blocking collectives: 76.2 us -> 62.8 us  [on_device(): lax.all_to_all(back.reshape(256, 16, 128), ('depth', 'rows'), split_axis=...]
    ppermute x6 -> x3, waiting for transfers between devices: 28.9 us -> 41.4 us  [exchange_kernel(): block = lax.ppermute(block, 'depth', [(d, d ^ e) for d in range(4)])]
    pallas_call x6 -> x3, Pallas kernels: 19.8 us -> 9.42 us  [the longest x1 4.14 us: on_device(): pl.pallas_call(column, grid=(2,), in_specs=[pl.BlockSpec(memory_space=plt...]
    all_to_all x2 -> x1, waiting for transfers between devices: 8.08 us -> 4.35 us  [on_device(): lax.all_to_all(send.reshape(256, 16, 128), ('depth', 'rows'), split_axis=...]
    ppermute x6 -> x3, starting transfers between devices: 6 us -> 3.45 us  [exchange_kernel(): block = lax.ppermute(block, 'depth', [(d, d ^ e) for d in range(4)])]
    all_to_all x2 -> x1, starting transfers between devices: 16.5 us -> 14.4 us  [on_device(): lax.all_to_all(send.reshape(256, 16, 128), ('depth', 'rows'), split_axis=...]
    unnamed x28 -> x22, local copies, waits for them, and re-layouts: 3.81 us -> 3.95 us
  transfers between devices with their start and end apart: 8 -> 4, of which waited for: 7 -> 3; matrix products, arithmetic and copies ran while one was open for 1% -> 1% of each run, Pallas kernels for 8% -> 1%
where the time goes in v1:
time: 151 us; the launch traced here: 150 us
  blocking collectives  62.8 us (42%)
  waiting for transfers between devices  45.7 us (30%)
  starting transfers between devices  17.8 us (12%)
  Pallas kernels  17.6 us (12%)
  local copies, waits for them, and re-layouts  5.63 us (4%)
    all_to_all x1, blocking collectives, on_device(): lax.all_to_all(back.reshape(256, 16, 128), ('depth', 'rows'), split_axis=...  62.8 us
    ppermute x3, waiting for transfers between devices, exchange_kernel(): block = lax.ppermute(block, 'depth', [(d, d ^ e) for d in range(4)])  41.4 us
    all_to_all x1, starting transfers between devices, on_device(): lax.all_to_all(send.reshape(256, 16, 128), ('depth', 'rows'), split_axis=...  14.4 us
    pallas_call x1, Pallas kernels, on_device(): pl.pallas_call(row_forward, grid=(steps,), in_specs=[pl.BlockSpec(memory_...  8.21 us
    all_to_all x1, waiting for transfers between devices, on_device(): lax.all_to_all(send.reshape(256, 16, 128), ('depth', 'rows'), split_axis=...  4.35 us
    pallas_call x1, Pallas kernels, on_device(): pl.pallas_call(column, grid=(2,), in_specs=[pl.BlockSpec(memory_space=plt...  4.14 us
    unnamed x22, local copies, waits for them, and re-layouts  3.95 us
    pallas_call x1, Pallas kernels, on_device(): pl.pallas_call(row_backward, grid=(steps,), in_specs=[row_block, whole((l...  3.51 us
  transfers between devices with their start and end apart: 4, of which 3 were waited for; matrix products, arithmetic and copies ran while one was open for 1% of the time, Pallas kernels for 1%

profile of v1, /device:TPU:32, one launch (start us, length us, event | category | flops | bytes accessed | tf_op | source)
XLA Modules:
  0.0 149.7 jit_solution(6593246979538849700)
XLA Ops:
  0.0 8.2 %row_forward.1 = (f32[128,4096]{1,0:T(8,128)}, f32[4096,128]{1,0:T(8,128)}) custom-call(f32[4]{0:T(128)} %contrasts.1, s32[128,4096]{1,0:T(8,128)} %bitcast.20, f32[128,4096]{1,0:T(8,128)} %bitcast.21, f32[128,4096]{1,0:T(8,128)} %bitcast.22, f32[16,2,128]{2,1,0:T(2,128)} %constant.38.clone.turn, bf16[256,768]{1,0:T(8,128)(2,1)} %constant.40.clone.pair, ...), custom_call_target="tpu_custom_call" | custom-call | flops 805306368 | bytes 12582912 | tf_op jit(solution)/shard_map/row_forward/pallas_call | solution.py:299
  8.2 14.4 %all-to-all-start = ((f32[256,16,128]{2,1,0:T(8,128)}), f32[256,16,128]{2,1,0:T(8,128)S(1)}, u32[]{:S(2)}, u32[]{:S(2)}) async-start(f32[256,16,128]{2,1,0:T(8,128)} %bitcast.23), calls=%async_computation | async-start | bytes 4194304 | tf_op jit(solution)/shard_map/all_to_all | solution.py:329
  22.6 1.7 %constant_dynamic-slice_fusion = (f32[2,16,4096]{2,1,0:T(8,128)S(1)}, f32[2,16,4096]{2,1,0:T(8,128)S(1)}, f32[2,16,4096]{2,1,0:T(8,128)S(1)}, f32[2,16,4096]{2,1,0:T(8,128)S(1)}) fusion(f32[2,64,4096]{2,1,0:T(8,128)} %param.19, s32[]{:T(128)S(6)} %select_n.15, s32[]{:T(128)S(6)} %select_n.14, s32[]{:T(128)S(6)} %select_n.13, s32[]{:T(128)S(6)} %select_n.12), kind=kLoop, calls=%fused_computation | loop fusion | bytes 4194320 | tf_op jit(solution)/shard_map/dynamic_slice | solution.py:282
  24.3 2.8 %collective-permute-start.2 = (f32[2,16,4096]{2,1,0:T(8,128)S(1)}, f32[2,16,4096]{2,1,0:T(8,128)S(1)}, u32[]{:S(2)}, u32[]{:S(2)}) collective-permute-start(f32[2,16,4096]{2,1,0:T(8,128)S(1)} %get-tuple-element.13), channel_id=1, source_target_pairs={{0,192},{64,128},{128,64},{192,0},{1,193},{65,129},{129,65},{193,1... | collective-permute-start | bytes 1572872 | tf_op jit(solution)/shard_map/ppermute | solution.py:284
  27.1 0.5 collective-permute-start.1
  27.7 0.1 collective-permute-start
  27.8 21.0 %collective-permute-done.2 = f32[2,16,4096]{2,1,0:T(8,128)S(1)} collective-permute-done((f32[2,16,4096]{2,1,0:T(8,128)S(1)}, f32[2,16,4096]{2,1,0:T(8,128)S(1)}, u32[]{:S(2)}, u32[]{:S(2)}) %collective-permute-start.2) | collective-permute-done | bytes 524320 | tf_op jit(solution)/shard_map/ppermute | solution.py:284
  48.7 20.4 %collective-permute-done.1 = f32[2,16,4096]{2,1,0:T(8,128)S(1)} collective-permute-done((f32[2,16,4096]{2,1,0:T(8,128)S(1)}, f32[2,16,4096]{2,1,0:T(8,128)S(1)}, u32[]{:S(2)}, u32[]{:S(2)}) %collective-permute-start.1) | collective-permute-done | bytes 524320 | tf_op jit(solution)/shard_map/ppermute | solution.py:284
  69.1 0.0 collective-permute-done
  69.1 0.0 copy-start.10
  69.2 1.8 %kernel_in_pairs.1.kernel = f32[4,32,16,256]{3,2,1,0:T(8,128)S(1)} custom-call(f32[32,4096]{1,0:T(8,128)S(1)} %bitcast.16, f32[32,4096]{1,0:T(8,128)S(1)} %bitcast.19, f32[32,4096]{1,0:T(8,128)S(1)} %bitcast.18, f32[32,4096]{1,0:T(8,128)S(1)} %bitcast.17), custom_call_target="tpu_custom_call" | custom-call | flops 2000000000 | bytes 4194304 | tf_op jit(solution)/shard_map/kernel_in_pairs/pallas_call | solution.py:332
  70.9 1.3 copy-done.1
  72.3 4.3 %all-to-all-done = f32[256,16,128]{2,1,0:T(8,128)S(1)} async-done(((f32[256,16,128]{2,1,0:T(8,128)}), f32[256,16,128]{2,1,0:T(8,128)S(1)}, u32[]{:S(2)}, u32[]{:S(2)}) %all-to-all-start) | async-done | bytes 2097184 | tf_op jit(solution)/shard_map/all_to_all | solution.py:329
  76.6 1.6 %copy-done.2 = f32[4,32,16,256]{3,2,1,0:T(8,128)S(1)} copy-done((f32[4,32,16,256]{3,2,1,0:T(8,128)S(1)}, f32[4,32,16,256]{3,2,1,0:T(8,128)}, u32[]{:S(2)}) %copy-start.2) | copy-done | bytes 2097176
  78.2 1.0 copy-done.6
  79.2 4.1 %column.1 = f32[4,64,16,128]{3,2,1,0:T(8,128)S(1)} custom-call(s32[1]{0:T(128)} %bitcast.3.place, f32[4,64,16,128]{3,2,1,0:T(8,128)S(1)} %bitcast.14, f32[4,32,16,256]{3,2,1,0:T(8,128)S(1)} %copy-done.2, f32[32,2,128]{2,1,0:T(2,128)S(1)} %copy-done.10, bf16[768,256]{1,0:T(8,128)(2,1)S(1)} %copy-done.6, bf16[768,256]{1,0:T(8,128)(2,1)S(1)} %copy-done.5, ...), custom_call_target="tpu_custom_call" | custom-call | flops 1610612736 | bytes 6291456 | tf_op jit(solution)/shard_map/column/pallas_call | solution.py:342
  83.4 0.0 copy-start
  83.4 0.0 copy-start.7
  83.4 0.0 copy-start.8
  83.4 0.0 copy-start.9
  83.4 62.8 %all_to_all.10 = f32[256,16,128]{2,1,0:T(8,128)S(1)} all-to-all(f32[256,16,128]{2,1,0:T(8,128)S(1)} %bitcast.15), channel_id=1, replica_groups=mesh['depth'=4,'rows'=64] {'depth','rows'}, dimensions={0} | all-to-all | bytes 4194304 | tf_op jit(solution)/shard_map/all_to_all | solution.py:366
  146.2 0.0 copy-done.8
  146.2 0.0 copy-done.9
  146.2 3.5 %row_backward.1 = f32[128,4096]{1,0:T(8,128)} custom-call(f32[128,4096]{1,0:T(8,128)S(1)} %copy-done, f32[4096,128]{1,0:T(8,128)S(1)} %bitcast.13, f32[16,2,128]{2,1,0:T(2,128)S(1)} %copy-done.9, bf16[768,256]{1,0:T(8,128)(2,1)S(1)} %copy-done.8, bf16[768,256]{1,0:T(8,128)(2,1)S(1)} %copy-done.7), custom_call_target="tpu_custom_call" | custom-call | flops 805306368 | bytes 6291456 | tf_op jit(solution)/shard_map/row_backward/pallas_call | solution.py:370
  (12 shorter events, 0.0 us)
Async XLA Ops:
  8.2 68.4 %all-to-all-start = ((f32[256,16,128]{2,1,0:T(8,128)}), f32[256,16,128]{2,1,0:T(8,128)S(1)}, u32[]{:S(2)}, u32[]{:S(2)}) async-start(f32[256,16,128]{2,1,0:T(8,128)} %bitcast.23), calls=%async_computation | async-start | bytes 4194304 | tf_op jit(solution)/shard_map/all_to_all | solution.py:329
  24.3 24.4 %collective-permute-start.2 = (f32[2,16,4096]{2,1,0:T(8,128)S(1)}, f32[2,16,4096]{2,1,0:T(8,128)S(1)}, u32[]{:S(2)}, u32[]{:S(2)}) collective-permute-start(f32[2,16,4096]{2,1,0:T(8,128)S(1)} %get-tuple-element.13), channel_id=1, source_target_pairs={{0,192},{64,128},{128,64},{192,0},{1,193},{65,129},{129,65},{193,1... | collective-permute-start | bytes 1572872 | tf_op jit(solution)/shard_map/ppermute | solution.py:284
  27.1 42.0 %collective-permute-start.1 = (f32[2,16,4096]{2,1,0:T(8,128)S(1)}, f32[2,16,4096]{2,1,0:T(8,128)S(1)}, u32[]{:S(2)}, u32[]{:S(2)}) collective-permute-start(f32[2,16,4096]{2,1,0:T(8,128)S(1)} %get-tuple-element.14), channel_id=1, source_target_pairs={{0,128},{64,192},{128,0},{192,64},{1,129},{65,193},{129,1},{193,65... | collective-permute-start | bytes 1572872 | tf_op jit(solution)/shard_map/ppermute | solution.py:284
  27.7 41.4 %collective-permute-start = (f32[2,16,4096]{2,1,0:T(8,128)S(1)}, f32[2,16,4096]{2,1,0:T(8,128)S(1)}, u32[]{:S(2)}, u32[]{:S(2)}) collective-permute-start(f32[2,16,4096]{2,1,0:T(8,128)S(1)} %get-tuple-element.15), channel_id=1, source_target_pairs={{0,64},{64,0},{128,192},{192,128},{1,65},{65,1},{129,193},{193,129... | collective-permute-start | bytes 1572872 | tf_op jit(solution)/shard_map/ppermute | solution.py:284
  69.1 7.5 %copy-start.3 = (bf16[768,256]{1,0:T(8,128)(2,1)S(1)}, bf16[768,256]{1,0:T(8,128)(2,1)}, u32[]{:S(2)}) copy-start(bf16[768,256]{1,0:T(8,128)(2,1)} %constant.45.clone.first_back) | copy-start | bytes 1179652
  69.1 7.5 %copy-start.4 = (bf16[768,256]{1,0:T(8,128)(2,1)S(1)}, bf16[768,256]{1,0:T(8,128)(2,1)}, u32[]{:S(2)}) copy-start(bf16[768,256]{1,0:T(8,128)(2,1)} %constant.44.clone.pair_back) | copy-start | bytes 1179652
  69.1 7.5 %copy-start.5 = (bf16[768,256]{1,0:T(8,128)(2,1)S(1)}, bf16[768,256]{1,0:T(8,128)(2,1)}, u32[]{:S(2)}) copy-start(bf16[768,256]{1,0:T(8,128)(2,1)} %constant.43.clone.first) | copy-start | bytes 1179652
  69.1 7.5 %copy-start.10 = (f32[32,2,128]{2,1,0:T(2,128)S(1)}, f32[32,2,128]{2,1,0:T(2,128)}, u32[]{:S(2)}) copy-start(f32[32,2,128]{2,1,0:T(2,128)} %constant.39.clone.turn) | copy-start | bytes 98308
  70.9 1.3 copy-start.1
  76.6 1.6 %copy-start.2 = (f32[4,32,16,256]{3,2,1,0:T(8,128)S(1)}, f32[4,32,16,256]{3,2,1,0:T(8,128)}, u32[]{:S(2)}) copy-start(f32[4,32,16,256]{3,2,1,0:T(8,128)} %copy-done.1) | copy-start | bytes 6291460
  78.2 1.0 copy-start.6
  83.4 62.8 %copy-start = (f32[128,4096]{1,0:T(8,128)S(1)}, f32[128,4096]{1,0:T(8,128)}, u32[]{:S(2)}) copy-start(f32[128,4096]{1,0:T(8,128)} %get-tuple-element.9.weight) | copy-start | bytes 6291460
  83.4 62.8 %copy-start.7 = (bf16[768,256]{1,0:T(8,128)(2,1)S(1)}, bf16[768,256]{1,0:T(8,128)(2,1)}, u32[]{:S(2)}) copy-start(bf16[768,256]{1,0:T(8,128)(2,1)} %constant.47.clone.first) | copy-start | bytes 1179652
  83.4 62.8 %copy-start.8 = (bf16[768,256]{1,0:T(8,128)(2,1)S(1)}, bf16[768,256]{1,0:T(8,128)(2,1)}, u32[]{:S(2)}) copy-start(bf16[768,256]{1,0:T(8,128)(2,1)} %constant.46.clone.pair) | copy-start | bytes 1179652
  83.4 62.8 %copy-start.9 = (f32[16,2,128]{2,1,0:T(2,128)S(1)}, f32[16,2,128]{2,1,0:T(2,128)}, u32[]{:S(2)}) copy-start(f32[16,2,128]{2,1,0:T(2,128)} %constant.38.clone.turn) | copy-start | bytes 49156

commit v2 on v1

--- a/solution.py
+++ b/solution.py
@@ -37,7 +37,7 @@
 
 
 def twiddles(small, wide):
-    k = np.arange(small // 2)[:, None]
+    k = np.arange(small // 2 + 1)[:, None]
     b = np.arange(wide)[None, :]
     angle = 2.0 * np.pi / (small * wide) * k * b
     return np.stack([np.cos(angle), -np.sin(angle)], axis=1).astype(np.float32)
@@ -120,48 +120,70 @@
     return pl.ds((2 * odd + k // 16) * 64 * 16 + k % 16, 64, stride=16)
 
 
-def row_forward(contrasts, labels, level_set, perturbation, turn, pair, first, weight, send, parts):
+def row_forward(contrasts, labels, level_set, perturbation, turn, pair, first, send, *scratch):
+    label_buf, level_buf, field_buf, turn_buf, pair_buf, first_buf, parts, block_sem, const_sem = scratch
+    copies = []
+    for step in range(steps):
+        rows = pl.ds(step * row_step, row_step)
+        for i, (source, into) in enumerate(
+            ((labels, label_buf), (level_set, level_buf), (perturbation, field_buf))
+        ):
+            copies.append(pltpu.make_async_copy(source.at[rows], into.at[rows], block_sem.at[i, step]))
+    constants = [
+        pltpu.make_async_copy(source, into, const_sem.at[i])
+        for i, (source, into) in enumerate(((turn, turn_buf), (pair, pair_buf), (first, first_buf)))
+    ]
+    constants[0].start()
+    for copy in copies:
+        copy.start()
+    for copy in constants[1:]:
+        copy.start()
+    scaled = [contrasts[unit] * (smoothing / math.pi) for unit in range(4)]
+    constants[0].wait()
+    for step in range(steps):
+        for copy in copies[3 * step : 3 * step + 3]:
+            copy.wait()
+
+        def tile_of(tile, carry):
+            rows = pl.ds(pl.multiple_of(step * row_step + tile * 8, 8), 8)
+            fields = []
+            for a in range(row_small):
+                at = (rows, pl.ds(a * row_wide, row_wide))
+                fields.append(unit_weight(scaled, label_buf[at], level_buf[at]) * field_buf[at])
+            spectrum = real_fft(fields)
+            parts[0, rows, :row_wide] = spectrum[0][0]
+            parts[0, rows, row_wide:] = spectrum[row_small // 2][0]
+            for k in range(1, row_small // 2):
+                re, im = spectrum[k]
+                c, s = turn_buf[k, 0:1, :], turn_buf[k, 1:2, :]
+                parts[k, rows, :row_wide] = re * c - im * s
+                parts[k, rows, row_wide:] = im * c + re * s
+            return carry
+
+        lax.fori_loop(0, row_step // 8, tile_of, 0)
+    for copy in constants[1:]:
+        copy.wait()
+    for k in range(row_small // 2):
+        value = split_value(parts[k], 1)
+        out = dot(value, (pair_buf if k else first_buf)[...], ((1,), (0,))).T
+        for half, place in enumerate((k, row_small - k if k else row_small // 2)):
+            for odd in range(2):
+                begin = (half * 2 + odd) * 64
+                send[block_rows(place, odd), :] = out[begin : begin + 64]
+
+
+def unit_weight(scaled, unit, level):
+    chosen = jnp.where(
+        unit < 2,
+        jnp.where(unit == 0, scaled[0], scaled[1]),
+        jnp.where(unit == 2, scaled[2], scaled[3]),
+    )
+    return chosen / (level * level + smoothing * smoothing)
+
+
+def row_backward(contrasts, labels, level_set, received, turn, pair, first, out, parts):
     step = pl.program_id(0)
     scaled = [contrasts[unit] * (smoothing / math.pi) for unit in range(4)]
-    for tile in range(row_step // 8):
-        rows = pl.ds(tile * 8, 8)
-        fields = []
-        for a in range(row_small):
-            at = (rows, pl.ds(a * row_wide, row_wide))
-            unit = labels[at]
-            chosen = jnp.where(
-                unit < 2,
-                jnp.where(unit == 0, scaled[0], scaled[1]),
-                jnp.where(unit == 2, scaled[2], scaled[3]),
-            )
-            level = level_set[at]
-            here = chosen / (level * level + smoothing * smoothing)
-            weight[at] = here
-            fields.append(here * perturbation[at])
-        spectrum = real_fft(fields)
-        into = pl.ds(pl.multiple_of(step * row_step + tile * 8, 8), 8)
-        parts[0, into, :row_wide] = spectrum[0][0]
-        parts[0, into, row_wide:] = spectrum[row_small // 2][0]
-        for k in range(1, row_small // 2):
-            re, im = spectrum[k]
-            c, s = turn[k, 0:1, :], turn[k, 1:2, :]
-            parts[k, into, :row_wide] = re * c - im * s
-            parts[k, into, row_wide:] = im * c + re * s
-
-    @pl.when(step == steps - 1)
-    def _():
-        for k in range(row_small // 2):
-            value = split_value(parts[k], 1)
-            matrix = (pair if k else first)[...]
-            out = dot(matrix, value, ((1,), (1,)))
-            for half, place in enumerate((k, row_small - k if k else row_small // 2)):
-                for odd in range(2):
-                    begin = (half * 2 + odd) * 64
-                    send[block_rows(place, odd), :] = out[begin : begin + 64]
-
-
-def row_backward(weight, received, turn, pair, first, out, parts):
-    step = pl.program_id(0)
 
     @pl.when(step == 0)
     def _():
@@ -190,39 +212,52 @@
         fields = real_fft_adjoint(spectrum)
         for a in range(row_small):
             at = (rows, pl.ds(a * row_wide, row_wide))
-            out[at] = fields[a] * weight[at]
-
-
-def column(place, received, kernel, turn, pair, first, pair_back, first_back, out, parts, data):
+            out[at] = fields[a] * unit_weight(scaled, labels[at], level_set[at])
+
+
+def column(place, received, kernel, turn, matrix, matrix_back, out, parts, data):
     half = col_small // 2
+    lanes = (slice(0, 64), slice(64, 128), slice(128, 192), slice(192, 256))
+    blank = jnp.zeros((8, 64), jnp.float32)
+    parts[:, half + 1] = jnp.zeros((4, 8, 256), jnp.float32)
     for e in range(4):
         source = place[0] ^ e
         spectrum = real_fft([received[source, r] for r in range(col_small)])
         parts[e, 0, :, :128] = spectrum[0][0]
-        parts[e, 0, :, 128:] = spectrum[half][0]
+        parts[e, 0, :, 128:] = jnp.zeros((8, 128), jnp.float32)
+        parts[e, half, :, :128] = spectrum[half][0] * turn[half, 0:1, :]
+        parts[e, half, :, 128:] = spectrum[half][0] * turn[half, 1:2, :]
         for k in range(1, half):
             re, im = spectrum[k]
             c, s = turn[k, 0:1, :], turn[k, 1:2, :]
             parts[e, k, :, :128] = re * c - im * s
             parts[e, k, :, 128:] = im * c + re * s
-        rest = dot(split_value(parts[e].reshape(half * 8, 256), 1), pair[...], ((1,), (0,)))
-        zero = dot(split_value(parts[e, 0], 1), first[...], ((1,), (0,)))
-        rest = rest.reshape(half, 8, 256)
+        value = split_value(parts[e].reshape(-1, 256), 1)
+        result = dot(value, matrix[...], ((1,), (0,))).reshape(half + 2, 8, 256)
+        zero, last = result[0], result[half]
+        first = jnp.concatenate(
+            [zero[:, lanes[0]], last[:, lanes[0]], zero[:, lanes[2]], last[:, lanes[2]]], axis=1
+        )
         for k in range(half):
-            spectra = (zero if k == 0 else rest[k]) * kernel[e, k]
+            spectra = (result[k] if k else first) * kernel[e, k]
             spectra = spectra[:, :128] + spectra[:, 128:]
             data[k] = spectra if e == 0 else data[k] + spectra
     for e in range(4):
-        scaled = jnp.concatenate([data[...], data[...]], axis=2) * kernel[e]
-        value = split_value(scaled.reshape(half * 8, 256), 1)
-        parts[e] = dot(value, pair_back[...], ((1,), (0,))).reshape(half, 8, 256)
-        parts[e, 0] = dot(split_value(scaled[0], 1), first_back[...], ((1,), (0,)))
+        for k in range(half):
+            scaled = jnp.concatenate([data[k], data[k]], axis=1) * kernel[e, k]
+            if k:
+                parts[e, k] = scaled
+            else:
+                low, high, low2, high2 = [scaled[:, at] for at in lanes]
+                parts[e, 0] = jnp.concatenate([low, blank, low2, blank], axis=1)
+                parts[e, half] = jnp.concatenate([high, blank, high2, blank], axis=1)
+        value = split_value(parts[e].reshape(-1, 256), 1)
+        parts[e] = dot(value, matrix_back[...], ((1,), (0,))).reshape(half + 2, 8, 256)
         spectrum = [(parts[e, 0, :, :128], None)]
-        for k in range(1, half):
+        for k in range(1, half + 1):
             tr, ti = parts[e, k, :, :128], parts[e, k, :, 128:]
             c, s = turn[k, 0:1, :], turn[k, 1:2, :]
-            spectrum.append((tr * c + ti * s, ti * c - tr * s))
-        spectrum.append((parts[e, 0, :, 128:], None))
+            spectrum.append((tr * c + ti * s, ti * c - tr * s if k < half else None))
         fields = real_fft_adjoint(spectrum)
         for r in range(col_small):
             out[place[0] ^ e, r] = fields[r]
@@ -240,15 +275,12 @@
     return pl.CostEstimate(flops=flops, bytes_accessed=moved, transcendentals=0)
 
 
-def column_matrices():
-    out = []
-    for matrix in stage_matrices(col_small, col_wide):
-        both = np.zeros((2, 2, col_wide, 2, 2, col_wide))
-        shaped = matrix.reshape(2, col_wide, 2, col_wide)
-        for layer in range(2):
-            both[layer, :, :, :, layer, :] = shaped
-        out.append(both.reshape(256, 256))
-    return out
+def column_matrix():
+    both = np.zeros((2, 2, col_wide, 2, 2, col_wide))
+    shaped = stage_matrices(col_small, col_wide)[0].reshape(2, col_wide, 2, col_wide)
+    for layer in range(2):
+        both[layer, :, :, :, layer, :] = shaped
+    return both.reshape(256, 256)
 
 
 def row_matrices():
@@ -293,27 +325,26 @@
     col_turn = twiddles(col_small, col_wide)
     col_turn = jnp.asarray(np.concatenate([col_turn, col_turn], axis=2))
     row_pair, row_first = row_matrices()
-    col_pair, col_first = column_matrices()
+    col_pair = column_matrix()
 
     row_block = pl.BlockSpec((row_step, length), lambda i: (i, 0))
-    weight, send = pl.pallas_call(
+    in_place = pl.BlockSpec(memory_space=pl.ANY)
+    scalars = pl.BlockSpec(memory_space=pltpu.SMEM)
+    send = pl.pallas_call(
         row_forward,
-        grid=(steps,),
-        in_specs=[
-            pl.BlockSpec(memory_space=pltpu.SMEM),
-            row_block,
-            row_block,
-            row_block,
-            whole((16, 2, 128)),
-            whole((256, 768)),
-            whole((256, 768)),
+        in_specs=[scalars] + [in_place] * 6,
+        out_shape=jax.ShapeDtypeStruct((length, 128), f32),
+        scratch_shapes=[
+            pltpu.VMEM((128, length), jnp.int32),
+            pltpu.VMEM((128, length), f32),
+            pltpu.VMEM((128, length), f32),
+            pltpu.VMEM((17, 2, 128), f32),
+            pltpu.VMEM((768, 256), bf16),
+            pltpu.VMEM((768, 256), bf16),
+            pltpu.VMEM((16, 128, 256), f32),
+            pltpu.SemaphoreType.DMA((3, steps)),
+            pltpu.SemaphoreType.DMA((3,)),
         ],
-        out_specs=[row_block, whole((length, 128))],
-        out_shape=[
-            jax.ShapeDtypeStruct((128, length), f32),
-            jax.ShapeDtypeStruct((length, 128), f32),
-        ],
-        scratch_shapes=[pltpu.VMEM((16, 128, 256), f32)],
         compiler_params=params(big),
         cost_estimate=cost(2 * 256 * 768 * 128 * 16, 12 * 2**20),
         name="row_forward",
@@ -321,11 +352,11 @@
         contrasts,
         *rows,
         row_turn,
-        jnp.asarray(split_matrix(row_pair, 1)),
-        jnp.asarray(split_matrix(row_first, 1)),
-    )
-
-    send, kernel = lax.optimization_barrier((send, kernel))
+        jnp.asarray(split_matrix(row_pair.T, 0)),
+        jnp.asarray(split_matrix(row_first.T, 0)),
+    )
+
+    send, kernel, later = lax.optimization_barrier((send, kernel, rows[:2]))
     received = lax.all_to_all(
         send.reshape(256, 16, 128), ("depth", "rows"), split_axis=0, concat_axis=0, tiled=True
     )
@@ -333,7 +364,7 @@
         kernel_in_pairs,
         out_shape=jax.ShapeDtypeStruct((4, 32, 16, 256), f32),
         scratch_shapes=[pltpu.VMEM((length, 128), f32)],
-        compiler_params=params(16),
+        compiler_params=params(12),
         cost_estimate=cost(2 * 10**9, 4 * 2**20),
         name="kernel_in_pairs",
     )(*exchange_kernel(kernel))
@@ -343,16 +374,17 @@
         column,
         grid=(2,),
         in_specs=[
-            pl.BlockSpec(memory_space=pltpu.SMEM),
+            scalars,
             block,
             pl.BlockSpec((4, 32, 8, 256), lambda i: (0, 0, i, 0)),
-            whole((32, 2, 128)),
-        ]
-        + [whole((768, 256))] * 4,
+            whole((33, 2, 128)),
+            whole((768, 256)),
+            whole((768, 256)),
+        ],
         out_specs=block,
         out_shape=jax.ShapeDtypeStruct((4, 64, 16, 128), f32),
-        scratch_shapes=[pltpu.VMEM((4, 32, 8, 256), f32), pltpu.VMEM((32, 8, 128), f32)],
-        compiler_params=params(32),
+        scratch_shapes=[pltpu.VMEM((4, 34, 8, 256), f32), pltpu.VMEM((32, 8, 128), f32)],
+        compiler_params=params(16),
         cost_estimate=cost(2 * 768 * 256 * 4096, 6 * 2**20),
         name="column",
     )(
@@ -360,8 +392,8 @@
         received.reshape(4, 64, 16, 128),
         kernels,
         col_turn,
-        *[jnp.asarray(split_matrix(m.T, 0)) for m in (col_pair, col_first)],
-        *[jnp.asarray(split_matrix(m, 0)) for m in (col_pair, col_first)],
+        jnp.asarray(split_matrix(col_pair.T, 0)),
+        jnp.asarray(split_matrix(col_pair, 0)),
     )
     returned = lax.all_to_all(
         back.reshape(256, 16, 128), ("depth", "rows"), split_axis=0, concat_axis=0, tiled=True
@@ -371,20 +403,23 @@
         row_backward,
         grid=(steps,),
         in_specs=[
+            scalars,
+            row_block,
             row_block,
             whole((length, 128)),
-            whole((16, 2, 128)),
+            whole((17, 2, 128)),
             whole((768, 256)),
             whole((768, 256)),
         ],
         out_specs=row_block,
         out_shape=jax.ShapeDtypeStruct((128, length), f32),
         scratch_shapes=[pltpu.VMEM((16, 128, 256), f32)],
-        compiler_params=params(24),
+        compiler_params=params(16),
         cost_estimate=cost(2 * 256 * 768 * 128 * 16, 6 * 2**20),
         name="row_backward",
     )(
-        weight,
+        contrasts,
+        *later,
         returned.reshape(length, 128),
         row_turn,
         jnp.asarray(split_matrix(row_pair, 0)),

time: 151 us -> 150 us (level)
  no operation moved by 1% of the time
where the time goes in v2:
time: 150 us; the launch traced here: 149 us
  blocking collectives  62.8 us (42%)
  waiting for transfers between devices  45.7 us (30%)
  starting transfers between devices  17.8 us (12%)
  Pallas kernels  17.7 us (12%)
  local copies, waits for them, and re-layouts  4.63 us (3%)
    all_to_all x1, blocking collectives, on_device(): lax.all_to_all(back.reshape(256, 16, 128), ('depth', 'rows'), split_axis=...  62.8 us
    ppermute x3, waiting for transfers between devices, exchange_kernel(): block = lax.ppermute(block, 'depth', [(d, d ^ e) for d in range(4)])  41.4 us
    all_to_all x1, starting transfers between devices, on_device(): lax.all_to_all(send.reshape(256, 16, 128), ('depth', 'rows'), split_axis=...  14.4 us
    pallas_call x1, Pallas kernels, on_device(): pl.pallas_call(row_forward, in_specs=[scalars] + [in_place] * 6, out_shap...  7.07 us
    pallas_call x1, Pallas kernels, on_device(): pl.pallas_call(row_backward, grid=(steps,), in_specs=[scalars, row_block,...  4.67 us
    all_to_all x1, waiting for transfers between devices, on_device(): lax.all_to_all(send.reshape(256, 16, 128), ('depth', 'rows'), split_axis=...  4.36 us
    pallas_call x1, Pallas kernels, on_device(): pl.pallas_call(column, grid=(2,), in_specs=[scalars, block, pl.BlockSpec(...  4.21 us
    ppermute x3, starting transfers between devices, exchange_kernel(): block = lax.ppermute(block, 'depth', [(d, d ^ e) for d in range(4)])  3.45 us
  transfers between devices with their start and end apart: 4, of which 3 were waited for; matrix products, arithmetic and copies ran while one was open for 1% of the time, Pallas kernels for 1%

profile of v2, /device:TPU:32, one launch (start us, length us, event | category | flops | bytes accessed | tf_op | source)
XLA Modules:
  0.0 148.8 jit_solution(17907718276331011096)
XLA Ops:
  0.0 7.1 %row_forward.1 = f32[4096,128]{1,0:T(8,128)} custom-call(f32[4]{0:T(128)} %contrasts.3, s32[128,4096]{1,0:T(8,128)} %bitcast.13, f32[128,4096]{1,0:T(8,128)} %bitcast.15, f32[128,4096]{1,0:T(8,128)} %bitcast.25, f32[17,2,128]{2,1,0:T(2,128)} %constant.34.clone.turn, bf16[768,256]{1,0:T(8,128)(2,1)} %constant.36.clone.pair, bf16[768,256]{1,0:T(8,128)(2,1)} %constant.37.clone.first), custom_call_target="tpu_custom_call" | custom-call | flops 805306368 | bytes 12582912 | tf_op jit(solution)/shard_map/row_forward/pallas_call | solution.py:333
  7.1 14.4 %all-to-all-start = ((f32[256,16,128]{2,1,0:T(8,128)}), f32[256,16,128]{2,1,0:T(8,128)S(1)}, u32[]{:S(2)}, u32[]{:S(2)}) async-start(f32[256,16,128]{2,1,0:T(8,128)} %bitcast.24), calls=%async_computation | async-start | bytes 4194304 | tf_op jit(solution)/shard_map/all_to_all | solution.py:360
  21.5 1.7 %constant_dynamic-slice_fusion = (f32[2,16,4096]{2,1,0:T(8,128)S(1)}, f32[2,16,4096]{2,1,0:T(8,128)S(1)}, f32[2,16,4096]{2,1,0:T(8,128)S(1)}, f32[2,16,4096]{2,1,0:T(8,128)S(1)}) fusion(f32[2,64,4096]{2,1,0:T(8,128)} %param.17, s32[]{:T(128)S(6)} %select_n.15, s32[]{:T(128)S(6)} %select_n.14, s32[]{:T(128)S(6)} %select_n.13, s32[]{:T(128)S(6)} %select_n.12), kind=kLoop, calls=%fused_computation | loop fusion | bytes 4194320 | tf_op jit(solution)/shard_map/dynamic_slice | solution.py:314
  23.2 2.8 %collective-permute-start.2 = (f32[2,16,4096]{2,1,0:T(8,128)S(1)}, f32[2,16,4096]{2,1,0:T(8,128)S(1)}, u32[]{:S(2)}, u32[]{:S(2)}) collective-permute-start(f32[2,16,4096]{2,1,0:T(8,128)S(1)} %get-tuple-element.13), channel_id=1, source_target_pairs={{0,192},{64,128},{128,64},{192,0},{1,193},{65,129},{129,65},{193,1... | collective-permute-start | bytes 1572872 | tf_op jit(solution)/shard_map/ppermute | solution.py:316
  26.0 0.5 collective-permute-start.1
  26.6 0.1 collective-permute-start
  26.6 21.0 %collective-permute-done.2 = f32[2,16,4096]{2,1,0:T(8,128)S(1)} collective-permute-done((f32[2,16,4096]{2,1,0:T(8,128)S(1)}, f32[2,16,4096]{2,1,0:T(8,128)S(1)}, u32[]{:S(2)}, u32[]{:S(2)}) %collective-permute-start.2) | collective-permute-done | bytes 524320 | tf_op jit(solution)/shard_map/ppermute | solution.py:316
  47.6 20.4 %collective-permute-done.1 = f32[2,16,4096]{2,1,0:T(8,128)S(1)} collective-permute-done((f32[2,16,4096]{2,1,0:T(8,128)S(1)}, f32[2,16,4096]{2,1,0:T(8,128)S(1)}, u32[]{:S(2)}, u32[]{:S(2)}) %collective-permute-start.1) | collective-permute-done | bytes 524320 | tf_op jit(solution)/shard_map/ppermute | solution.py:316
  68.0 0.0 collective-permute-done
  68.0 1.8 %kernel_in_pairs.1.kernel = f32[4,32,16,256]{3,2,1,0:T(8,128)S(1)} custom-call(f32[32,4096]{1,0:T(8,128)S(1)} %bitcast.20, f32[32,4096]{1,0:T(8,128)S(1)} %bitcast.23, f32[32,4096]{1,0:T(8,128)S(1)} %bitcast.22, f32[32,4096]{1,0:T(8,128)S(1)} %bitcast.21), custom_call_target="tpu_custom_call" | custom-call | flops 2000000000 | bytes 4194304 | tf_op jit(solution)/shard_map/kernel_in_pairs/pallas_call | solution.py:363
  69.8 1.3 copy-done.2
  71.1 4.4 %all-to-all-done = f32[256,16,128]{2,1,0:T(8,128)S(1)} async-done(((f32[256,16,128]{2,1,0:T(8,128)}), f32[256,16,128]{2,1,0:T(8,128)S(1)}, u32[]{:S(2)}, u32[]{:S(2)}) %all-to-all-start) | async-done | bytes 2097184 | tf_op jit(solution)/shard_map/all_to_all | solution.py:360
  75.5 0.0 copy-done.6
  75.5 0.0 copy-done.7
  75.5 0.0 copy-done.9
  75.5 0.0 copy-start.3
  75.5 1.6 %copy-done.3 = f32[4,32,16,256]{3,2,1,0:T(8,128)S(1)} copy-done((f32[4,32,16,256]{3,2,1,0:T(8,128)S(1)}, f32[4,32,16,256]{3,2,1,0:T(8,128)}, u32[]{:S(2)}) %copy-start.3) | copy-done | bytes 2097176
  77.1 4.2 %column.1 = f32[4,64,16,128]{3,2,1,0:T(8,128)S(1)} custom-call(s32[1]{0:T(128)} %bitcast.3.place, f32[4,64,16,128]{3,2,1,0:T(8,128)S(1)} %bitcast.18, f32[4,32,16,256]{3,2,1,0:T(8,128)S(1)} %copy-done.3, f32[33,2,128]{2,1,0:T(2,128)S(1)} %copy-done.9, bf16[768,256]{1,0:T(8,128)(2,1)S(1)} %copy-done.7, bf16[768,256]{1,0:T(8,128)(2,1)S(1)} %copy-done.6), custom_call_target="tpu_custom_call" | custom-call | flops 1610612736 | bytes 6291456 | tf_op jit(solution)/shard_map/column/pallas_call | solution.py:373
  81.3 0.0 copy-start
  81.3 0.0 copy-start.1
  81.3 0.0 copy-start.10
  81.3 62.8 %all_to_all.10 = f32[256,16,128]{2,1,0:T(8,128)S(1)} all-to-all(f32[256,16,128]{2,1,0:T(8,128)S(1)} %bitcast.19), channel_id=1, replica_groups=mesh['depth'=4,'rows'=64] {'depth','rows'}, dimensions={0} | all-to-all | bytes 4194304 | tf_op jit(solution)/shard_map/all_to_all | solution.py:398
  144.1 0.0 copy-done.5
  144.2 4.7 %row_backward.1 = f32[128,4096]{1,0:T(8,128)} custom-call(f32[4]{0:T(128)S(1)} %copy-done.10, s32[128,4096]{1,0:T(8,128)S(1)} %bitcast.14, f32[128,4096]{1,0:T(8,128)S(1)} %bitcast.16, f32[4096,128]{1,0:T(8,128)S(1)} %bitcast.17, f32[17,2,128]{2,1,0:T(2,128)S(1)} %copy-done.8, bf16[768,256]{1,0:T(8,128)(2,1)S(1)} %copy-done.5, bf16[768,256]{1,0:T(8,128)(2,1)S(1)} %copy-done.4), custom_call_target="tpu_custom_call" | custom-call | flops 805306368 | bytes 6291456 | tf_op jit(solution)/shard_map/row_backward/pallas_call | solution.py:402
  (12 shorter events, 0.0 us)
Async XLA Ops:
  7.1 68.4 %all-to-all-start = ((f32[256,16,128]{2,1,0:T(8,128)}), f32[256,16,128]{2,1,0:T(8,128)S(1)}, u32[]{:S(2)}, u32[]{:S(2)}) async-start(f32[256,16,128]{2,1,0:T(8,128)} %bitcast.24), calls=%async_computation | async-start | bytes 4194304 | tf_op jit(solution)/shard_map/all_to_all | solution.py:360
  23.2 24.4 %collective-permute-start.2 = (f32[2,16,4096]{2,1,0:T(8,128)S(1)}, f32[2,16,4096]{2,1,0:T(8,128)S(1)}, u32[]{:S(2)}, u32[]{:S(2)}) collective-permute-start(f32[2,16,4096]{2,1,0:T(8,128)S(1)} %get-tuple-element.13), channel_id=1, source_target_pairs={{0,192},{64,128},{128,64},{192,0},{1,193},{65,129},{129,65},{193,1... | collective-permute-start | bytes 1572872 | tf_op jit(solution)/shard_map/ppermute | solution.py:316
  26.0 42.0 %collective-permute-start.1 = (f32[2,16,4096]{2,1,0:T(8,128)S(1)}, f32[2,16,4096]{2,1,0:T(8,128)S(1)}, u32[]{:S(2)}, u32[]{:S(2)}) collective-permute-start(f32[2,16,4096]{2,1,0:T(8,128)S(1)} %get-tuple-element.14), channel_id=1, source_target_pairs={{0,128},{64,192},{128,0},{192,64},{1,129},{65,193},{129,1},{193,65... | collective-permute-start | bytes 1572872 | tf_op jit(solution)/shard_map/ppermute | solution.py:316
  26.6 41.4 %collective-permute-start = (f32[2,16,4096]{2,1,0:T(8,128)S(1)}, f32[2,16,4096]{2,1,0:T(8,128)S(1)}, u32[]{:S(2)}, u32[]{:S(2)}) collective-permute-start(f32[2,16,4096]{2,1,0:T(8,128)S(1)} %get-tuple-element.15), channel_id=1, source_target_pairs={{0,64},{64,0},{128,192},{192,128},{1,65},{65,1},{129,193},{193,129... | collective-permute-start | bytes 1572872 | tf_op jit(solution)/shard_map/ppermute | solution.py:316
  68.0 7.5 %copy-start.6 = (bf16[768,256]{1,0:T(8,128)(2,1)S(1)}, bf16[768,256]{1,0:T(8,128)(2,1)}, u32[]{:S(2)}) copy-start(bf16[768,256]{1,0:T(8,128)(2,1)} %constant.39.clone.matrix_back) | copy-start | bytes 1179652
  68.0 7.5 %copy-start.7 = (bf16[768,256]{1,0:T(8,128)(2,1)S(1)}, bf16[768,256]{1,0:T(8,128)(2,1)}, u32[]{:S(2)}) copy-start(bf16[768,256]{1,0:T(8,128)(2,1)} %constant.38.clone.matrix) | copy-start | bytes 1179652
  68.0 7.5 %copy-start.9 = (f32[33,2,128]{2,1,0:T(2,128)S(1)}, f32[33,2,128]{2,1,0:T(2,128)}, u32[]{:S(2)}) copy-start(f32[33,2,128]{2,1,0:T(2,128)} %constant.35.clone.turn) | copy-start | bytes 101380
  69.8 1.3 copy-start.2
  75.5 1.6 %copy-start.3 = (f32[4,32,16,256]{3,2,1,0:T(8,128)S(1)}, f32[4,32,16,256]{3,2,1,0:T(8,128)}, u32[]{:S(2)}) copy-start(f32[4,32,16,256]{3,2,1,0:T(8,128)} %copy-done.2) | copy-start | bytes 6291460
  77.1 67.0 %copy-start.4 = (bf16[768,256]{1,0:T(8,128)(2,1)S(1)}, bf16[768,256]{1,0:T(8,128)(2,1)}, u32[]{:S(2)}) copy-start(bf16[768,256]{1,0:T(8,128)(2,1)} %constant.41.clone.first) | copy-start | bytes 1179652
  77.1 67.0 %copy-start.5 = (bf16[768,256]{1,0:T(8,128)(2,1)S(1)}, bf16[768,256]{1,0:T(8,128)(2,1)}, u32[]{:S(2)}) copy-start(bf16[768,256]{1,0:T(8,128)(2,1)} %constant.40.clone.pair) | copy-start | bytes 1179652
  77.1 67.0 %copy-start.8 = (f32[17,2,128]{2,1,0:T(2,128)S(1)}, f32[17,2,128]{2,1,0:T(2,128)}, u32[]{:S(2)}) copy-start(f32[17,2,128]{2,1,0:T(2,128)} %constant.34.clone.turn) | copy-start | bytes 52228
  81.3 62.8 %copy-start = (s32[2,64,4096]{2,1,0:T(8,128)S(1)}, s32[2,64,4096]{2,1,0:T(8,128)}, u32[]{:S(2)}) copy-start(s32[2,64,4096]{2,1,0:T(8,128)} %param.15) | copy-start | bytes 6291460
  81.3 62.8 %copy-start.1 = (f32[2,64,4096]{2,1,0:T(8,128)S(1)}, f32[2,64,4096]{2,1,0:T(8,128)}, u32[]{:S(2)}) copy-start(f32[2,64,4096]{2,1,0:T(8,128)} %param.14) | copy-start | bytes 6291460
  81.3 62.8 %copy-start.10 = (f32[4]{0:T(128)S(1)}, f32[4]{0:T(128)}, u32[]{:S(2)}) copy-start(f32[4]{0:T(128)} %contrasts.3) | copy-start | bytes 52

commit v3 on v2

--- a/solution.py
+++ b/solution.py
@@ -112,7 +112,7 @@
 
 row_small, row_wide = 32, 128
 col_small, col_wide = 64, 64
-row_step = 32
+row_step = 64
 steps = 128 // row_step
 
 

time: 150 us -> 149 us (level)
  no operation moved by 1% of the time
where the time goes in v3:
time: 149 us
  blocking collectives  62.8 us (42%)
  waiting for transfers between devices  45.7 us (31%)
  starting transfers between devices  17.8 us (12%)
  Pallas kernels  17.4 us (12%)
  local copies, waits for them, and re-layouts  4.63 us (3%)
    all_to_all x1, blocking collectives, on_device(): lax.all_to_all(back.reshape(256, 16, 128), ('depth', 'rows'), split_axis=...  62.8 us
    ppermute x3, waiting for transfers between devices, exchange_kernel(): block = lax.ppermute(block, 'depth', [(d, d ^ e) for d in range(4)])  41.4 us
    all_to_all x1, starting transfers between devices, on_device(): lax.all_to_all(send.reshape(256, 16, 128), ('depth', 'rows'), split_axis=...  14.4 us
    pallas_call x1, Pallas kernels, on_device(): pl.pallas_call(row_forward, in_specs=[scalars] + [in_place] * 6, out_shap...  7.06 us
    pallas_call x1, Pallas kernels, on_device(): pl.pallas_call(row_backward, grid=(steps,), in_specs=[scalars, row_block,...  4.41 us
    all_to_all x1, waiting for transfers between devices, on_device(): lax.all_to_all(send.reshape(256, 16, 128), ('depth', 'rows'), split_axis=...  4.36 us
    pallas_call x1, Pallas kernels, on_device(): pl.pallas_call(column, grid=(2,), in_specs=[scalars, block, pl.BlockSpec(...  4.21 us
    ppermute x3, starting transfers between devices, exchange_kernel(): block = lax.ppermute(block, 'depth', [(d, d ^ e) for d in range(4)])  3.45 us
  transfers between devices with their start and end apart: 4, of which 3 were waited for; matrix products, arithmetic and copies ran while one was open for 1% of the time, Pallas kernels for 1%

profile of v3, /device:TPU:32, one launch (start us, length us, event | category | flops | bytes accessed | tf_op | source)
XLA Modules:
  0.0 148.6 jit_solution(11420938035421329478)
XLA Ops:
  0.0 7.1 %row_forward.1 = f32[4096,128]{1,0:T(8,128)} custom-call(f32[4]{0:T(128)} %contrasts.3, s32[128,4096]{1,0:T(8,128)} %bitcast.13, f32[128,4096]{1,0:T(8,128)} %bitcast.15, f32[128,4096]{1,0:T(8,128)} %bitcast.25, f32[17,2,128]{2,1,0:T(2,128)} %constant.34.clone.turn, bf16[768,256]{1,0:T(8,128)(2,1)} %constant.36.clone.pair, bf16[768,256]{1,0:T(8,128)(2,1)} %constant.37.clone.first), custom_call_target="tpu_custom_call" | custom-call | flops 805306368 | bytes 12582912 | tf_op jit(solution)/shard_map/row_forward/pallas_call | solution.py:333
  7.1 14.4 %all-to-all-start = ((f32[256,16,128]{2,1,0:T(8,128)}), f32[256,16,128]{2,1,0:T(8,128)S(1)}, u32[]{:S(2)}, u32[]{:S(2)}) async-start(f32[256,16,128]{2,1,0:T(8,128)} %bitcast.24), calls=%async_computation | async-start | bytes 4194304 | tf_op jit(solution)/shard_map/all_to_all | solution.py:360
  21.5 1.7 %constant_dynamic-slice_fusion = (f32[2,16,4096]{2,1,0:T(8,128)S(1)}, f32[2,16,4096]{2,1,0:T(8,128)S(1)}, f32[2,16,4096]{2,1,0:T(8,128)S(1)}, f32[2,16,4096]{2,1,0:T(8,128)S(1)}) fusion(f32[2,64,4096]{2,1,0:T(8,128)} %param.17, s32[]{:T(128)S(6)} %select_n.15, s32[]{:T(128)S(6)} %select_n.14, s32[]{:T(128)S(6)} %select_n.13, s32[]{:T(128)S(6)} %select_n.12), kind=kLoop, calls=%fused_computation | loop fusion | bytes 4194320 | tf_op jit(solution)/shard_map/dynamic_slice | solution.py:314
  23.2 2.8 %collective-permute-start.2 = (f32[2,16,4096]{2,1,0:T(8,128)S(1)}, f32[2,16,4096]{2,1,0:T(8,128)S(1)}, u32[]{:S(2)}, u32[]{:S(2)}) collective-permute-start(f32[2,16,4096]{2,1,0:T(8,128)S(1)} %get-tuple-element.13), channel_id=1, source_target_pairs={{0,192},{64,128},{128,64},{192,0},{1,193},{65,129},{129,65},{193,1... | collective-permute-start | bytes 1572872 | tf_op jit(solution)/shard_map/ppermute | solution.py:316
  26.0 0.5 collective-permute-start.1
  26.6 0.1 collective-permute-start
  26.6 21.0 %collective-permute-done.2 = f32[2,16,4096]{2,1,0:T(8,128)S(1)} collective-permute-done((f32[2,16,4096]{2,1,0:T(8,128)S(1)}, f32[2,16,4096]{2,1,0:T(8,128)S(1)}, u32[]{:S(2)}, u32[]{:S(2)}) %collective-permute-start.2) | collective-permute-done | bytes 524320 | tf_op jit(solution)/shard_map/ppermute | solution.py:316
  47.6 20.4 %collective-permute-done.1 = f32[2,16,4096]{2,1,0:T(8,128)S(1)} collective-permute-done((f32[2,16,4096]{2,1,0:T(8,128)S(1)}, f32[2,16,4096]{2,1,0:T(8,128)S(1)}, u32[]{:S(2)}, u32[]{:S(2)}) %collective-permute-start.1) | collective-permute-done | bytes 524320 | tf_op jit(solution)/shard_map/ppermute | solution.py:316
  68.0 0.0 collective-permute-done
  68.0 1.8 %kernel_in_pairs.1.kernel = f32[4,32,16,256]{3,2,1,0:T(8,128)S(1)} custom-call(f32[32,4096]{1,0:T(8,128)S(1)} %bitcast.20, f32[32,4096]{1,0:T(8,128)S(1)} %bitcast.23, f32[32,4096]{1,0:T(8,128)S(1)} %bitcast.22, f32[32,4096]{1,0:T(8,128)S(1)} %bitcast.21), custom_call_target="tpu_custom_call" | custom-call | flops 2000000000 | bytes 4194304 | tf_op jit(solution)/shard_map/kernel_in_pairs/pallas_call | solution.py:363
  69.8 1.3 copy-done.2
  71.1 4.4 %all-to-all-done = f32[256,16,128]{2,1,0:T(8,128)S(1)} async-done(((f32[256,16,128]{2,1,0:T(8,128)}), f32[256,16,128]{2,1,0:T(8,128)S(1)}, u32[]{:S(2)}, u32[]{:S(2)}) %all-to-all-start) | async-done | bytes 2097184 | tf_op jit(solution)/shard_map/all_to_all | solution.py:360
  75.5 0.0 copy-done.6
  75.5 0.0 copy-done.7
  75.5 0.0 copy-done.9
  75.5 0.0 copy-start.3
  75.5 1.6 %copy-done.3 = f32[4,32,16,256]{3,2,1,0:T(8,128)S(1)} copy-done((f32[4,32,16,256]{3,2,1,0:T(8,128)S(1)}, f32[4,32,16,256]{3,2,1,0:T(8,128)}, u32[]{:S(2)}) %copy-start.3) | copy-done | bytes 2097176
  77.1 4.2 %column.1 = f32[4,64,16,128]{3,2,1,0:T(8,128)S(1)} custom-call(s32[1]{0:T(128)} %bitcast.3.place, f32[4,64,16,128]{3,2,1,0:T(8,128)S(1)} %bitcast.18, f32[4,32,16,256]{3,2,1,0:T(8,128)S(1)} %copy-done.3, f32[33,2,128]{2,1,0:T(2,128)S(1)} %copy-done.9, bf16[768,256]{1,0:T(8,128)(2,1)S(1)} %copy-done.7, bf16[768,256]{1,0:T(8,128)(2,1)S(1)} %copy-done.6), custom_call_target="tpu_custom_call" | custom-call | flops 1610612736 | bytes 6291456 | tf_op jit(solution)/shard_map/column/pallas_call | solution.py:373
  81.3 0.0 copy-start
  81.3 0.0 copy-start.1
  81.3 0.0 copy-start.10
  81.3 62.8 %all_to_all.10 = f32[256,16,128]{2,1,0:T(8,128)S(1)} all-to-all(f32[256,16,128]{2,1,0:T(8,128)S(1)} %bitcast.19), channel_id=1, replica_groups=mesh['depth'=4,'rows'=64] {'depth','rows'}, dimensions={0} | all-to-all | bytes 4194304 | tf_op jit(solution)/shard_map/all_to_all | solution.py:398
  144.1 0.0 copy-done.5
  144.2 4.4 %row_backward.1 = f32[128,4096]{1,0:T(8,128)} custom-call(f32[4]{0:T(128)S(1)} %copy-done.10, s32[128,4096]{1,0:T(8,128)S(1)} %bitcast.14, f32[128,4096]{1,0:T(8,128)S(1)} %bitcast.16, f32[4096,128]{1,0:T(8,128)S(1)} %bitcast.17, f32[17,2,128]{2,1,0:T(2,128)S(1)} %copy-done.8, bf16[768,256]{1,0:T(8,128)(2,1)S(1)} %copy-done.5, bf16[768,256]{1,0:T(8,128)(2,1)S(1)} %copy-done.4), custom_call_target="tpu_custom_call" | custom-call | flops 805306368 | bytes 6291456 | tf_op jit(solution)/shard_map/row_backward/pallas_call | solution.py:402
  (12 shorter events, 0.0 us)
Async XLA Ops:
  7.1 68.4 %all-to-all-start = ((f32[256,16,128]{2,1,0:T(8,128)}), f32[256,16,128]{2,1,0:T(8,128)S(1)}, u32[]{:S(2)}, u32[]{:S(2)}) async-start(f32[256,16,128]{2,1,0:T(8,128)} %bitcast.24), calls=%async_computation | async-start | bytes 4194304 | tf_op jit(solution)/shard_map/all_to_all | solution.py:360
  23.2 24.4 %collective-permute-start.2 = (f32[2,16,4096]{2,1,0:T(8,128)S(1)}, f32[2,16,4096]{2,1,0:T(8,128)S(1)}, u32[]{:S(2)}, u32[]{:S(2)}) collective-permute-start(f32[2,16,4096]{2,1,0:T(8,128)S(1)} %get-tuple-element.13), channel_id=1, source_target_pairs={{0,192},{64,128},{128,64},{192,0},{1,193},{65,129},{129,65},{193,1... | collective-permute-start | bytes 1572872 | tf_op jit(solution)/shard_map/ppermute | solution.py:316
  26.0 42.0 %collective-permute-start.1 = (f32[2,16,4096]{2,1,0:T(8,128)S(1)}, f32[2,16,4096]{2,1,0:T(8,128)S(1)}, u32[]{:S(2)}, u32[]{:S(2)}) collective-permute-start(f32[2,16,4096]{2,1,0:T(8,128)S(1)} %get-tuple-element.14), channel_id=1, source_target_pairs={{0,128},{64,192},{128,0},{192,64},{1,129},{65,193},{129,1},{193,65... | collective-permute-start | bytes 1572872 | tf_op jit(solution)/shard_map/ppermute | solution.py:316
  26.6 41.4 %collective-permute-start = (f32[2,16,4096]{2,1,0:T(8,128)S(1)}, f32[2,16,4096]{2,1,0:T(8,128)S(1)}, u32[]{:S(2)}, u32[]{:S(2)}) collective-permute-start(f32[2,16,4096]{2,1,0:T(8,128)S(1)} %get-tuple-element.15), channel_id=1, source_target_pairs={{0,64},{64,0},{128,192},{192,128},{1,65},{65,1},{129,193},{193,129... | collective-permute-start | bytes 1572872 | tf_op jit(solution)/shard_map/ppermute | solution.py:316
  68.0 7.5 %copy-start.6 = (bf16[768,256]{1,0:T(8,128)(2,1)S(1)}, bf16[768,256]{1,0:T(8,128)(2,1)}, u32[]{:S(2)}) copy-start(bf16[768,256]{1,0:T(8,128)(2,1)} %constant.39.clone.matrix_back) | copy-start | bytes 1179652
  68.0 7.5 %copy-start.7 = (bf16[768,256]{1,0:T(8,128)(2,1)S(1)}, bf16[768,256]{1,0:T(8,128)(2,1)}, u32[]{:S(2)}) copy-start(bf16[768,256]{1,0:T(8,128)(2,1)} %constant.38.clone.matrix) | copy-start | bytes 1179652
  68.0 7.5 %copy-start.9 = (f32[33,2,128]{2,1,0:T(2,128)S(1)}, f32[33,2,128]{2,1,0:T(2,128)}, u32[]{:S(2)}) copy-start(f32[33,2,128]{2,1,0:T(2,128)} %constant.35.clone.turn) | copy-start | bytes 101380
  69.8 1.3 copy-start.2
  75.5 1.6 %copy-start.3 = (f32[4,32,16,256]{3,2,1,0:T(8,128)S(1)}, f32[4,32,16,256]{3,2,1,0:T(8,128)}, u32[]{:S(2)}) copy-start(f32[4,32,16,256]{3,2,1,0:T(8,128)} %copy-done.2) | copy-start | bytes 6291460
  77.1 67.0 %copy-start.4 = (bf16[768,256]{1,0:T(8,128)(2,1)S(1)}, bf16[768,256]{1,0:T(8,128)(2,1)}, u32[]{:S(2)}) copy-start(bf16[768,256]{1,0:T(8,128)(2,1)} %constant.41.clone.first) | copy-start | bytes 1179652
  77.1 67.0 %copy-start.5 = (bf16[768,256]{1,0:T(8,128)(2,1)S(1)}, bf16[768,256]{1,0:T(8,128)(2,1)}, u32[]{:S(2)}) copy-start(bf16[768,256]{1,0:T(8,128)(2,1)} %constant.40.clone.pair) | copy-start | bytes 1179652
  77.1 67.0 %copy-start.8 = (f32[17,2,128]{2,1,0:T(2,128)S(1)}, f32[17,2,128]{2,1,0:T(2,128)}, u32[]{:S(2)}) copy-start(f32[17,2,128]{2,1,0:T(2,128)} %constant.34.clone.turn) | copy-start | bytes 52228
  81.3 62.8 %copy-start = (s32[2,64,4096]{2,1,0:T(8,128)S(1)}, s32[2,64,4096]{2,1,0:T(8,128)}, u32[]{:S(2)}) copy-start(s32[2,64,4096]{2,1,0:T(8,128)} %param.15) | copy-start | bytes 6291460
  81.3 62.8 %copy-start.1 = (f32[2,64,4096]{2,1,0:T(8,128)S(1)}, f32[2,64,4096]{2,1,0:T(8,128)}, u32[]{:S(2)}) copy-start(f32[2,64,4096]{2,1,0:T(8,128)} %param.14) | copy-start | bytes 6291460
  81.3 62.8 %copy-start.10 = (f32[4]{0:T(128)S(1)}, f32[4]{0:T(128)}, u32[]{:S(2)}) copy-start(f32[4]{0:T(128)} %contrasts.3) | copy-start | bytes 52

commit v4 on v2

--- a/solution.py
+++ b/solution.py
@@ -215,8 +215,9 @@
             out[at] = fields[a] * unit_weight(scaled, labels[at], level_set[at])
 
 
-def column(place, received, kernel, turn, matrix, matrix_back, out, parts, data):
+def column(place, received, early, late, turn, matrix, matrix_back, out, parts, data):
     half = col_small // 2
+    kernel = (early.at[0], early.at[1], late.at[0], early.at[2])
     lanes = (slice(0, 64), slice(64, 128), slice(128, 192), slice(192, 256))
     blank = jnp.zeros((8, 64), jnp.float32)
     parts[:, half + 1] = jnp.zeros((4, 8, 256), jnp.float32)
@@ -239,12 +240,12 @@
             [zero[:, lanes[0]], last[:, lanes[0]], zero[:, lanes[2]], last[:, lanes[2]]], axis=1
         )
         for k in range(half):
-            spectra = (result[k] if k else first) * kernel[e, k]
+            spectra = (result[k] if k else first) * kernel[e][k]
             spectra = spectra[:, :128] + spectra[:, 128:]
             data[k] = spectra if e == 0 else data[k] + spectra
     for e in range(4):
         for k in range(half):
-            scaled = jnp.concatenate([data[k], data[k]], axis=1) * kernel[e, k]
+            scaled = jnp.concatenate([data[k], data[k]], axis=1) * kernel[e][k]
             if k:
                 parts[e, k] = scaled
             else:
@@ -292,7 +293,7 @@
 
 
 def kernel_in_pairs(*refs):
-    sources, out, turned = refs[:4], refs[4], refs[5]
+    sources, out, turned = refs[:-2], refs[-2], refs[-1]
     for tile in range(length // 128):
         lanes = pl.ds(tile * 128, 128)
         turned[lanes, :] = jnp.concatenate([x[:, lanes] for x in sources], axis=0).T
@@ -301,7 +302,7 @@
         pair = jnp.concatenate(
             [turned[pl.ds(place, col_wide, stride=col_small), :] for place in places], axis=0
         ).T
-        for e in range(4):
+        for e in range(len(sources)):
             for layer in range(2):
                 begin = e * 32 + layer * 16
                 out[e, k, :, layer * 128 : layer * 128 + 128] = pair[begin : begin + 16]
@@ -360,14 +361,18 @@
     received = lax.all_to_all(
         send.reshape(256, 16, 128), ("depth", "rows"), split_axis=0, concat_axis=0, tiled=True
     )
-    kernels = pl.pallas_call(
-        kernel_in_pairs,
-        out_shape=jax.ShapeDtypeStruct((4, 32, 16, 256), f32),
-        scratch_shapes=[pltpu.VMEM((length, 128), f32)],
-        compiler_params=params(12),
-        cost_estimate=cost(2 * 10**9, 4 * 2**20),
-        name="kernel_in_pairs",
-    )(*exchange_kernel(kernel))
+    def in_pairs(*sources):
+        return pl.pallas_call(
+            kernel_in_pairs,
+            out_shape=jax.ShapeDtypeStruct((len(sources), 32, 16, 256), f32),
+            scratch_shapes=[pltpu.VMEM((length, 32 * len(sources)), f32)],
+            compiler_params=params(12),
+            cost_estimate=cost(10**9, 2 * 2**20),
+            name="kernel_in_pairs",
+        )(*sources)
+
+    blocks = exchange_kernel(kernel)
+    early, late = in_pairs(blocks[0], blocks[1], blocks[3]), in_pairs(blocks[2])
 
     block = pl.BlockSpec((4, 64, 8, 128), lambda i: (0, 0, i, 0))
     back = pl.pallas_call(
@@ -376,7 +381,8 @@
         in_specs=[
             scalars,
             block,
-            pl.BlockSpec((4, 32, 8, 256), lambda i: (0, 0, i, 0)),
+            pl.BlockSpec((3, 32, 8, 256), lambda i: (0, 0, i, 0)),
+            pl.BlockSpec((1, 32, 8, 256), lambda i: (0, 0, i, 0)),
             whole((33, 2, 128)),
             whole((768, 256)),
             whole((768, 256)),
@@ -390,7 +396,8 @@
     )(
         lax.axis_index("depth").reshape(1),
         received.reshape(4, 64, 16, 128),
-        kernels,
+        early,
+        late,
         col_turn,
         jnp.asarray(split_matrix(col_pair.T, 0)),
         jnp.asarray(split_matrix(col_pair, 0)),

time: 150 us -> 149 us (level)
  waiting for transfers between devices: 45.7 us -> 43.8 us
  Pallas kernels: 17.7 us -> 19.6 us
    ppermute x3, waiting for transfers between devices: 41.4 us -> 38.1 us  [exchange_kernel(): block = lax.ppermute(block, 'depth', [(d, d ^ e) for d in range(4)])]
    pallas_call x1 -> x2, Pallas kernels: 1.76 us -> 3.56 us  [in_pairs(): pl.pallas_call(kernel_in_pairs, out_shape=jax.ShapeDtypeStruct((len(sourc...]
  transfers between devices with their start and end apart: 4 -> 4, of which waited for: 3 -> 3; matrix products, arithmetic and copies ran while one was open for 1% -> 1% of each run, Pallas kernels for 1% -> 2%
where the time goes in v4:
time: 149 us; the launch traced here: 148 us
  blocking collectives  62.2 us (42%)
  waiting for transfers between devices  43.8 us (29%)
  Pallas kernels  19.6 us (13%)
  starting transfers between devices  18.1 us (12%)
  local copies, waits for them, and re-layouts  4.3 us (3%)
    all_to_all x1, blocking collectives, on_device(): lax.all_to_all(back.reshape(256, 16, 128), ('depth', 'rows'), split_axis=...  62.2 us
    ppermute x3, waiting for transfers between devices, exchange_kernel(): block = lax.ppermute(block, 'depth', [(d, d ^ e) for d in range(4)])  38.1 us
    all_to_all x1, starting transfers between devices, on_device(): lax.all_to_all(send.reshape(256, 16, 128), ('depth', 'rows'), split_axis=...  14.4 us
    pallas_call x1, Pallas kernels, on_device(): pl.pallas_call(row_forward, in_specs=[scalars] + [in_place] * 6, out_shap...  7.13 us
    all_to_all x1, waiting for transfers between devices, on_device(): lax.all_to_all(send.reshape(256, 16, 128), ('depth', 'rows'), split_axis=...  5.65 us
    pallas_call x1, Pallas kernels, on_device(): pl.pallas_call(row_backward, grid=(steps,), in_specs=[scalars, row_block,...  4.67 us
    pallas_call x1, Pallas kernels, on_device(): pl.pallas_call(column, grid=(2,), in_specs=[scalars, block, pl.BlockSpec(...  4.21 us
    ppermute x3, starting transfers between devices, exchange_kernel(): block = lax.ppermute(block, 'depth', [(d, d ^ e) for d in range(4)])  3.73 us
  transfers between devices with their start and end apart: 4, of which 3 were waited for; matrix products, arithmetic and copies ran while one was open for 1% of the time, Pallas kernels for 2%

profile of v4, /device:TPU:32, one launch (start us, length us, event | category | flops | bytes accessed | tf_op | source)
XLA Modules:
  0.0 148.1 jit_solution(5254059317191323774)
XLA Ops:
  0.0 7.1 %row_forward.1 = f32[4096,128]{1,0:T(8,128)} custom-call(f32[4]{0:T(128)} %contrasts.3, s32[128,4096]{1,0:T(8,128)} %bitcast.13, f32[128,4096]{1,0:T(8,128)} %bitcast.15, f32[128,4096]{1,0:T(8,128)} %bitcast.25, f32[17,2,128]{2,1,0:T(2,128)} %constant.34.clone.turn, bf16[768,256]{1,0:T(8,128)(2,1)} %constant.36.clone.pair, bf16[768,256]{1,0:T(8,128)(2,1)} %constant.37.clone.first), custom_call_target="tpu_custom_call" | custom-call | flops 805306368 | bytes 12582912 | tf_op jit(solution)/shard_map/row_forward/pallas_call | solution.py:334
  7.1 14.4 %all-to-all-start = ((f32[256,16,128]{2,1,0:T(8,128)}), f32[256,16,128]{2,1,0:T(8,128)S(1)}, u32[]{:S(2)}, u32[]{:S(2)}) async-start(f32[256,16,128]{2,1,0:T(8,128)} %bitcast.24), calls=%async_computation | async-start | bytes 4194304 | tf_op jit(solution)/shard_map/all_to_all | solution.py:361
  21.6 1.7 %constant_dynamic-slice_fusion = (f32[2,16,4096]{2,1,0:T(8,128)S(1)}, f32[2,16,4096]{2,1,0:T(8,128)S(1)}, f32[2,16,4096]{2,1,0:T(8,128)S(1)}, f32[2,16,4096]{2,1,0:T(8,128)S(1)}) fusion(f32[2,64,4096]{2,1,0:T(8,128)} %param.17, s32[]{:T(128)S(6)} %select_n.15, s32[]{:T(128)S(6)} %select_n.14, s32[]{:T(128)S(6)} %select_n.13, s32[]{:T(128)S(6)} %select_n.12), kind=kLoop, calls=%fused_computation | loop fusion | bytes 4194320 | tf_op jit(solution)/shard_map/dynamic_slice | solution.py:315
  23.3 3.1 %collective-permute-start.2 = (f32[2,16,4096]{2,1,0:T(8,128)S(1)}, f32[2,16,4096]{2,1,0:T(8,128)S(1)}, u32[]{:S(2)}, u32[]{:S(2)}) collective-permute-start(f32[2,16,4096]{2,1,0:T(8,128)S(1)} %get-tuple-element.13), channel_id=1, source_target_pairs={{0,128},{64,192},{128,0},{192,64},{1,129},{65,193},{129,1},{193,65... | collective-permute-start | bytes 1572872 | tf_op jit(solution)/shard_map/ppermute | solution.py:317
  26.3 0.0 collective-permute-start.1
  26.4 0.6 collective-permute-start
  27.0 21.9 %collective-permute-done.2 = f32[2,16,4096]{2,1,0:T(8,128)S(1)} collective-permute-done((f32[2,16,4096]{2,1,0:T(8,128)S(1)}, f32[2,16,4096]{2,1,0:T(8,128)S(1)}, u32[]{:S(2)}, u32[]{:S(2)}) %collective-permute-start.2) | collective-permute-done | bytes 524320 | tf_op jit(solution)/shard_map/ppermute | solution.py:317
  48.9 1.8 %kernel_in_pairs.3.late = f32[1,32,16,256]{3,2,1,0:T(8,128)S(1)} custom-call(f32[32,4096]{1,0:T(8,128)S(1)} %bitcast.23), custom_call_target="tpu_custom_call" | custom-call | flops 1000000000 | bytes 2097152 | tf_op jit(solution)/shard_map/kernel_in_pairs/pallas_call | solution.py:365
  50.7 0.0 copy-start.9
  50.7 16.2 %collective-permute-done.1 = f32[2,16,4096]{2,1,0:T(8,128)S(1)} collective-permute-done((f32[2,16,4096]{2,1,0:T(8,128)S(1)}, f32[2,16,4096]{2,1,0:T(8,128)S(1)}, u32[]{:S(2)}, u32[]{:S(2)}) %collective-permute-start.1) | collective-permute-done | bytes 524320 | tf_op jit(solution)/shard_map/ppermute | solution.py:317
  66.9 0.0 collective-permute-done
  66.9 1.8 %kernel_in_pairs.2.early = f32[3,32,16,256]{3,2,1,0:T(8,128)S(1)} custom-call(f32[32,4096]{1,0:T(8,128)S(1)} %bitcast.20, f32[32,4096]{1,0:T(8,128)S(1)} %bitcast.22, f32[32,4096]{1,0:T(8,128)S(1)} %bitcast.21), custom_call_target="tpu_custom_call" | custom-call | flops 1000000000 | bytes 2097152 | tf_op jit(solution)/shard_map/kernel_in_pairs/pallas_call | solution.py:365
  68.7 1.2 copy-done.2
  69.9 5.7 %all-to-all-done = f32[256,16,128]{2,1,0:T(8,128)S(1)} async-done(((f32[256,16,128]{2,1,0:T(8,128)}), f32[256,16,128]{2,1,0:T(8,128)S(1)}, u32[]{:S(2)}, u32[]{:S(2)}) %all-to-all-start) | async-done | bytes 2097184 | tf_op jit(solution)/shard_map/all_to_all | solution.py:361
  75.5 0.0 copy-done.6
  75.6 1.4 copy-done.3
  77.0 4.2 %column.1 = f32[4,64,16,128]{3,2,1,0:T(8,128)S(1)} custom-call(s32[1]{0:T(128)} %bitcast.3.place, f32[4,64,16,128]{3,2,1,0:T(8,128)S(1)} %bitcast.18, f32[3,32,16,256]{3,2,1,0:T(8,128)S(1)} %copy-done.3, f32[1,32,16,256]{3,2,1,0:T(8,128)S(1)} %kernel_in_pairs.3.late, f32[33,2,128]{2,1,0:T(2,128)S(1)} %copy-done.9, bf16[768,256]{1,0:T(8,128)(2,1)S(1)} %copy-done.7, ...), custom_call_target="tpu_custom_call" | custom-call | flops 1610612736 | bytes 6291456 | tf_op jit(solution)/shard_map/column/pallas_call | solution.py:378
  81.2 0.0 copy-start
  81.2 0.0 copy-start.1
  81.2 0.0 copy-start.10
  81.2 62.2 %all_to_all.10 = f32[256,16,128]{2,1,0:T(8,128)S(1)} all-to-all(f32[256,16,128]{2,1,0:T(8,128)S(1)} %bitcast.19), channel_id=1, replica_groups=mesh['depth'=4,'rows'=64] {'depth','rows'}, dimensions={0} | all-to-all | bytes 4194304 | tf_op jit(solution)/shard_map/all_to_all | solution.py:405
  143.4 0.0 copy-done.4
  143.4 0.0 copy-done.8
  143.4 4.7 %row_backward.1 = f32[128,4096]{1,0:T(8,128)} custom-call(f32[4]{0:T(128)S(1)} %copy-done.10, s32[128,4096]{1,0:T(8,128)S(1)} %bitcast.14, f32[128,4096]{1,0:T(8,128)S(1)} %bitcast.16, f32[4096,128]{1,0:T(8,128)S(1)} %bitcast.17, f32[17,2,128]{2,1,0:T(2,128)S(1)} %copy-done.8, bf16[768,256]{1,0:T(8,128)(2,1)S(1)} %copy-done.5, bf16[768,256]{1,0:T(8,128)(2,1)S(1)} %copy-done.4), custom_call_target="tpu_custom_call" | custom-call | flops 805306368 | bytes 6291456 | tf_op jit(solution)/shard_map/row_backward/pallas_call | solution.py:409
  (13 shorter events, 0.0 us)
Async XLA Ops:
  7.1 68.4 %all-to-all-start = ((f32[256,16,128]{2,1,0:T(8,128)}), f32[256,16,128]{2,1,0:T(8,128)S(1)}, u32[]{:S(2)}, u32[]{:S(2)}) async-start(f32[256,16,128]{2,1,0:T(8,128)} %bitcast.24), calls=%async_computation | async-start | bytes 4194304 | tf_op jit(solution)/shard_map/all_to_all | solution.py:361
  23.3 25.7 %collective-permute-start.2 = (f32[2,16,4096]{2,1,0:T(8,128)S(1)}, f32[2,16,4096]{2,1,0:T(8,128)S(1)}, u32[]{:S(2)}, u32[]{:S(2)}) collective-permute-start(f32[2,16,4096]{2,1,0:T(8,128)S(1)} %get-tuple-element.13), channel_id=1, source_target_pairs={{0,128},{64,192},{128,0},{192,64},{1,129},{65,193},{129,1},{193,65... | collective-permute-start | bytes 1572872 | tf_op jit(solution)/shard_map/ppermute | solution.py:317
  26.3 40.6 %collective-permute-start.1 = (f32[2,16,4096]{2,1,0:T(8,128)S(1)}, f32[2,16,4096]{2,1,0:T(8,128)S(1)}, u32[]{:S(2)}, u32[]{:S(2)}) collective-permute-start(f32[2,16,4096]{2,1,0:T(8,128)S(1)} %get-tuple-element.14), channel_id=1, source_target_pairs={{0,192},{64,128},{128,64},{192,0},{1,193},{65,129},{129,65},{193,1... | collective-permute-start | bytes 1572872 | tf_op jit(solution)/shard_map/ppermute | solution.py:317
  26.4 40.5 %collective-permute-start = (f32[2,16,4096]{2,1,0:T(8,128)S(1)}, f32[2,16,4096]{2,1,0:T(8,128)S(1)}, u32[]{:S(2)}, u32[]{:S(2)}) collective-permute-start(f32[2,16,4096]{2,1,0:T(8,128)S(1)} %get-tuple-element.15), channel_id=1, source_target_pairs={{0,64},{64,0},{128,192},{192,128},{1,65},{65,1},{129,193},{193,129... | collective-permute-start | bytes 1572872 | tf_op jit(solution)/shard_map/ppermute | solution.py:317
  50.7 24.9 %copy-start.6 = (bf16[768,256]{1,0:T(8,128)(2,1)S(1)}, bf16[768,256]{1,0:T(8,128)(2,1)}, u32[]{:S(2)}) copy-start(bf16[768,256]{1,0:T(8,128)(2,1)} %constant.39.clone.matrix_back) | copy-start | bytes 1179652
  50.7 24.9 %copy-start.7 = (bf16[768,256]{1,0:T(8,128)(2,1)S(1)}, bf16[768,256]{1,0:T(8,128)(2,1)}, u32[]{:S(2)}) copy-start(bf16[768,256]{1,0:T(8,128)(2,1)} %constant.38.clone.matrix) | copy-start | bytes 1179652
  50.7 24.8 %copy-start.9 = (f32[33,2,128]{2,1,0:T(2,128)S(1)}, f32[33,2,128]{2,1,0:T(2,128)}, u32[]{:S(2)}) copy-start(f32[33,2,128]{2,1,0:T(2,128)} %constant.35.clone.turn) | copy-start | bytes 101380
  68.7 1.2 copy-start.2
  75.6 1.4 copy-start.3
  77.0 66.4 %copy-start.4 = (bf16[768,256]{1,0:T(8,128)(2,1)S(1)}, bf16[768,256]{1,0:T(8,128)(2,1)}, u32[]{:S(2)}) copy-start(bf16[768,256]{1,0:T(8,128)(2,1)} %constant.41.clone.first) | copy-start | bytes 1179652
  77.0 66.4 %copy-start.5 = (bf16[768,256]{1,0:T(8,128)(2,1)S(1)}, bf16[768,256]{1,0:T(8,128)(2,1)}, u32[]{:S(2)}) copy-start(bf16[768,256]{1,0:T(8,128)(2,1)} %constant.40.clone.pair) | copy-start | bytes 1179652
  77.0 66.4 %copy-start.8 = (f32[17,2,128]{2,1,0:T(2,128)S(1)}, f32[17,2,128]{2,1,0:T(2,128)}, u32[]{:S(2)}) copy-start(f32[17,2,128]{2,1,0:T(2,128)} %constant.34.clone.turn) | copy-start | bytes 52228
  81.2 62.2 %copy-start = (s32[2,64,4096]{2,1,0:T(8,128)S(1)}, s32[2,64,4096]{2,1,0:T(8,128)}, u32[]{:S(2)}) copy-start(s32[2,64,4096]{2,1,0:T(8,128)} %param.15) | copy-start | bytes 6291460
  81.2 62.2 %copy-start.1 = (f32[2,64,4096]{2,1,0:T(8,128)S(1)}, f32[2,64,4096]{2,1,0:T(8,128)}, u32[]{:S(2)}) copy-start(f32[2,64,4096]{2,1,0:T(8,128)} %param.14) | copy-start | bytes 6291460
  81.2 62.2 %copy-start.10 = (f32[4]{0:T(128)S(1)}, f32[4]{0:T(128)}, u32[]{:S(2)}) copy-start(f32[4]{0:T(128)} %contrasts.3) | copy-start | bytes 52
